TPU v7x, 256 devices: a whole 4x4x8 slice. The times are simulated.
256 devices in a mesh: seq: 32 (over z, x), head: 8 (over y, core).
Axes of the slice: x: 4, y: 4, z: 8, core: 2. Of those that a mesh axis runs over, the one named last changes fastest.
Arguments:
- embedding: bfloat16 [8192, 4096], P('seq', 'head'), may hold values from -6 to 6
- noise_draw: bfloat16 [8192, 4096], P('seq', 'head'), may hold values from -3 to 3
- weight_x: bfloat16 [4096, 4096], P(None, 'head'), may hold values from -0.09375 to 0.09375
- weight_z: bfloat16 [4096, 4096], P(None, 'head'), may hold values from -0.09375 to 0.09375
- b_proj: float32 [8192, 128], P('seq'), may hold values from -0.015625 to 0.015625
- c_proj: float32 [8192, 128], P('seq'), may hold values from -6 to 6
- log_decay: float32 [64, 8192], P('head', 'seq'), may hold values from -1.3 to 0, as said below
- skip_gain: float32 [64], P('head'), may hold values from 0.5 to 1.5
- class_weight: bfloat16 [4096, 32], P('head'), may hold values from -6 to 6
- true_label: int32 [8192], P('seq'), may hold values from 0 to 31
Outputs:
- emb_grad: float32 [8192, 4096], P('seq', 'head')
Inputs may be any that keep to these rules, and one draw needn't show every extreme that they name: `log_decay`: each entry is the logarithm of one head's decay factor at one token.
All inputs are finite; a program needn't handle non-finite values.
Results may differ from a plain program's by a relative error of at most 0.02.
Values may be sent and summed in bfloat16 or wider, within the bound.
A program may use at most 128 MiB of HBM per device.

v0:
```python
import jax
import jax.numpy as jnp
from jax import lax
from jax.sharding import PartitionSpec as P

SPAN = 256


precise = lax.Precision.HIGHEST


def entering(value, axis, join, neutral, backward):
    count = lax.axis_size(axis)
    place = lax.axis_index(axis)
    ahead = count - 1 - place if backward else place
    gathered = jax.tree.map(
        lambda a, kind: lax.all_gather(a.astype(kind), axis), value, (jnp.bfloat16, jnp.bfloat16)
    )
    state = jax.tree.map(lambda a, e: jnp.zeros_like(a) + jnp.asarray(e, a.dtype), value, neutral)

    def one(lap, state):
        source = count - 1 - lap if backward else lap
        return join(
            state,
            jax.tree.map(
                lambda a, own: lax.dynamic_index_in_dim(a, source, 0, False).astype(own.dtype),
                gathered,
                value,
            ),
        )

    return lax.fori_loop(0, ahead, one, state)


def span_weights(local_cum, c_block, b_block):
    scores = jnp.einsum("tn,sn->ts", c_block, b_block, precision=precise)
    cum_heads = local_cum.T
    spread = cum_heads[:, :, None] - cum_heads[:, None, :]
    block_width = local_cum.shape[0]
    lower = jnp.arange(block_width)[:, None] >= jnp.arange(block_width)[None, :]
    return jnp.where(lower[None, :, :], jnp.exp(jnp.minimum(spread, 0.0)), 0.0) * scores[None, :, :]


def local_forward(x_blocks, cum_blocks, b_blocks, c_blocks, weights_all, zero_state):

    def block_step(carried, block_data):
        x_block, local_cum, b_block, c_block, weights = block_data
        output = jnp.einsum("hts,shp->thp", weights, x_block, precision=precise)
        output = output + jnp.exp(local_cum)[:, :, None] * jnp.einsum(
            "tn,hpn->thp", c_block, carried, precision=precise
        )
        final_cum = local_cum[-1]
        carried = jnp.exp(final_cum)[:, None, None] * carried + jnp.einsum(
            "sh,shp,sn->hpn",
            jnp.exp(final_cum[None, :] - local_cum),
            x_block,
            b_block,
            precision=precise,
        )
        return (carried, output)

    return lax.scan(block_step, zero_state, (x_blocks, cum_blocks, b_blocks, c_blocks, weights_all))


def local_backward(g_blocks, cum_blocks, b_blocks, c_blocks, weights_all, zero_state):

    def block_step(carried, block_data):
        g_block, local_cum, b_block, c_block, weights = block_data
        final_cum = local_cum[-1]
        output = jnp.einsum("hts,thp->shp", weights, g_block, precision=precise)
        output = output + jnp.exp(final_cum[None, :] - local_cum)[:, :, None] * jnp.einsum(
            "sn,hpn->shp", b_block, carried, precision=precise
        )
        carried = jnp.exp(final_cum)[:, None, None] * carried + jnp.einsum(
            "th,thp,tn->hpn", jnp.exp(local_cum), g_block, c_block, precision=precise
        )
        return (carried, output)

    return lax.scan(
        block_step,
        zero_state,
        (g_blocks, cum_blocks, b_blocks, c_blocks, weights_all),
        reverse=True,
    )


def forward_combine(earlier_part, later_part):
    return (
        earlier_part[0] + later_part[0],
        jnp.exp(later_part[0])[..., None, None] * earlier_part[1] + later_part[1],
    )


def backward_combine(earlier_part, later_part):
    return (
        earlier_part[0] + later_part[0],
        later_part[1] + jnp.exp(later_part[0])[..., None, None] * earlier_part[1],
    )


def local(
    embedding,
    noise_draw,
    weight_x,
    weight_z,
    b_proj,
    c_proj,
    log_decay,
    skip_gain,
    class_weight,
    true_label,
):
    mixed = (embedding.astype(jnp.float32) + noise_draw.astype(jnp.float32)).astype(jnp.bfloat16)
    tok_count = mixed.shape[0]
    inner_width = weight_x.shape[1]
    head_count = skip_gain.shape[0]
    head_dim = inner_width // head_count
    state_dim = b_proj.shape[1]
    shard_piece = lax.all_gather(mixed, "head", axis=1, tiled=True)
    rows_x = weight_x
    rows_z = weight_z
    x_inner = jnp.dot(shard_piece, rows_x, preferred_element_type=jnp.float32)
    z_inner = jnp.dot(shard_piece, rows_z, preferred_element_type=jnp.float32)
    rates_tok = log_decay.T
    block_width = min(SPAN, tok_count)
    number_of_blocks = tok_count // block_width
    cum_rates = jnp.cumsum(rates_tok, axis=0)
    device_total = cum_rates[-1]
    cum_blocks = jnp.cumsum(rates_tok.reshape(number_of_blocks, block_width, head_count), axis=1)
    b_blocks = b_proj.reshape(number_of_blocks, block_width, state_dim)
    c_blocks = c_proj.reshape(number_of_blocks, block_width, state_dim)
    weights_all = jax.vmap(span_weights)(cum_blocks, c_blocks, b_blocks)
    zero_state = jnp.zeros((head_count, head_dim, state_dim), jnp.float32)
    x_heads = x_inner.reshape(tok_count, head_count, head_dim)
    end_state, y_blocks = local_forward(
        x_heads.reshape(number_of_blocks, block_width, head_count, head_dim),
        cum_blocks,
        b_blocks,
        c_blocks,
        weights_all,
        zero_state,
    )
    onehot = (
        true_label[:, None] == jnp.arange(class_weight.shape[1], dtype=jnp.int32)[None, :]
    ).astype(jnp.bfloat16)
    columns = lax.dot_general(
        onehot, class_weight, (((1,), (1,)), ((), ())), preferred_element_type=jnp.float32
    )
    sigmoid_z = jax.nn.sigmoid(z_inner)
    grad_y = columns * (z_inner * sigmoid_z)
    grad_heads = grad_y.reshape(tok_count, head_count, head_dim)
    grad_begin, dx_blocks = local_backward(
        grad_heads.reshape(number_of_blocks, block_width, head_count, head_dim),
        cum_blocks,
        b_blocks,
        c_blocks,
        weights_all,
        zero_state,
    )
    zero_rates = jnp.zeros((head_count,), jnp.float32)
    state_in = entering(
        (device_total, end_state), "seq", forward_combine, (zero_rates, zero_state), False
    )[1]
    grad_in = entering(
        (device_total, grad_begin), "seq", backward_combine, (zero_rates, zero_state), True
    )[1]
    output_y = y_blocks.reshape(tok_count, head_count, head_dim)
    output_y = output_y + jnp.exp(cum_rates)[:, :, None] * jnp.einsum(
        "tn,hpn->thp", c_proj, state_in, precision=precise
    )
    output_y = (output_y + skip_gain[None, :, None] * x_heads).reshape(tok_count, inner_width)
    grad_z = (columns * output_y * sigmoid_z * (1.0 + z_inner * (1.0 - sigmoid_z))).astype(
        jnp.bfloat16
    )
    grad_x = dx_blocks.reshape(tok_count, head_count, head_dim)
    grad_x = grad_x + jnp.exp(device_total[None, :] - cum_rates)[:, :, None] * jnp.einsum(
        "sn,hpn->shp", b_proj, grad_in, precision=precise
    )
    grad_x = (
        (grad_x + skip_gain[None, :, None] * grad_heads)
        .reshape(tok_count, inner_width)
        .astype(jnp.bfloat16)
    )
    rows_x = weight_x
    rows_z = weight_z
    contract = (((1,), (1,)), ((), ()))
    term_x = lax.dot_general(rows_x, grad_x, contract, preferred_element_type=jnp.float32)
    term_z = lax.dot_general(rows_z, grad_z, contract, preferred_element_type=jnp.float32)
    grad_cols = lax.psum_scatter(
        (term_x + term_z).astype(jnp.bfloat16), "head", scatter_dimension=0, tiled=True
    ).astype(jnp.float32)
    return grad_cols.T


def solution(mesh):
    return jax.shard_map(
        local,
        mesh=mesh,
        in_specs=(
            P("seq", "head"),
            P("seq", "head"),
            P(None, "head"),
            P(None, "head"),
            P("seq", None),
            P("seq", None),
            P("head", "seq"),
            P("head"),
            P("head", None),
            P("seq"),
        ),
        out_specs=P("seq", "head"),
        check_vma=False,
    )
```

profile of v0, /device:TPU:1, one launch (start us, length us, event | category | flops | bytes accessed | tf_op | source)
XLA Modules:
  0.0 287.1 jit_solution(16230970553292971517)
XLA Ops:
  6.5 1.8 add_convert_fusion
  8.4 1.3 reduce-window.14
  9.7 0.2 slice_reduce_fusion.1
  10.0 0.2 slice_reduce_fusion.2
  10.2 0.1 fusion.44
  10.3 31.0 %all-gather.7.cloned.1.call-done = bf16[256,4096]{1,0:T(8,128)(2,1)} async-done(((bf16[256,512]{1,0:T(8,128)(2,1)}), bf16[256,4096]{1,0:T(8,128)(2,1)}) %all-gather.7.cloned.1.call-update) | async-done | bytes 2097168 | tf_op jit(solution)/shard_map/all_gather | solution.py:119
  41.3 4.6 %fusion.56 = f32[256,512]{0,1:T(8,128)S(1)} fusion(bf16[256,4096]{1,0:T(8,128)(2,1)} %all-gather.7.cloned.1.call-done, bf16[4096,512]{1,0:T(8,128)(2,1)} %param.16), kind=kOutput, calls=%fused_computation.89 | convolution fusion | flops 1073741824 | bytes 6815744 | tf_op jit(solution)/shard_map/dot_general | solution.py:122
  45.8 1.2 fusion.18
  47.1 4.1 %fusion.53 = f32[256,512]{1,0:T(8,128)S(1)} fusion(bf16[256,4096]{1,0:T(8,128)(2,1)} %all-gather.7.cloned.1.call-done, bf16[4096,512]{1,0:T(8,128)(2,1)} %param.17), kind=kOutput, calls=%fused_computation.86 | convolution fusion | flops 1073741824 | bytes 6815744 | tf_op jit(solution)/shard_map/dot_general | solution.py:123
  51.2 0.3 multiply_multiply_fusion
  51.5 0.2 copy.33
  51.8 1.2 fusion.17
  53.1 0.6 reduce-window.16
  53.7 0.2 slice_reduce_fusion
  53.9 0.1 fusion.52
  54.0 0.2 fusion.46
  54.1 34.2 %all-gather.2 = bf16[32,1,8]{2,1,0:T(2,128)(2,1)S(1)} all-gather(bf16[1,1,8]{2,1,0:T(2,128)(2,1)S(1)} %bitcast.154), channel_id=1, replica_groups=mesh['seq'=32,'head'=8] {'seq'}, dimensions={0}, use_global_device_ids=true | all-gather | bytes 528 | tf_op jit(solution)/shard_map/all_gather | solution.py:17
  88.3 0.2 slice_reduce_fusion.3
  88.7 0.4 fusion.54
  89.1 3.3 %fusion.5 = f32[256,8,64]{0,2,1:T(8,128)} fusion(f32[256,8,64]{0,2,1:T(8,128)S(1)} %bitcast.144, f32[256,256]{1,0:T(8,128)S(1)} %fusion.54, f32[8,256]{1,0:T(8,128)S(1)} %bitcast_add_fusion.1, pred[256,256]{1,0:T(8,128)(4,1)S(1)} %iota_compare_fusion), kind=kOutput, calls=%fused_computation.11 | convolution fusion | flops 404750336 | bytes 1384448 | tf_op jit(solution)/shard_map/while/body/eval_jaxpr/hts,shp->thp/dot_general | solution.py:48
  92.4 1.9 fusion.4
  94.3 32.0 %all-gather.11.cloned.1.call-done = bf16[256,64,128]{2,1,0:T(8,128)(2,1)} async-done(((bf16[8,64,128]{2,1,0:T(8,128)(2,1)}), bf16[256,64,128]{2,1,0:T(8,128)(2,1)}) %all-gather.11.cloned.1.call-update) | async-done | bytes 4194320 | tf_op jit(solution)/shard_map/all_gather | solution.py:17
  126.3 0.6 fusion.15
  126.9 1.7 fusion.14
  128.6 0.2 copy.38
  128.8 79.2 %all-gather.9.cloned.1.call-done = bf16[256,64,128]{2,1,0:T(8,128)(2,1)} async-done(((bf16[8,64,128]{2,1,0:T(8,128)(2,1)}), bf16[256,64,128]{2,1,0:T(8,128)(2,1)}) %all-gather.9.cloned.1.call-update) | async-done | bytes 4194320 | tf_op jit(solution)/shard_map/all_gather | solution.py:17
  208.0 33.0 %while.16 = (s32[]{:T(128)}, f32[8,64,128]{2,1,0:T(8,128)S(1)}, s32[]{:T(128)}, bf16[32,8,64,128]{3,2,1,0:T(8,128)(2,1)}, bf16[32,8]{1,0:T(8,128)(2,1)S(1)}, /*index=5*/s32[]{:T(128)}, s32[]{:T(128)}, s32[]{:T(128)}, s32[]{:T(128)}) while((s32[]{:T(128)}, f32[8,64,128]{2,1,0:T(8,128)S(1)}, s32[]{:T(128)}, bf16[32,8,64,128]{3,2,1,0:T(8,128)(2,1)}, ...), condition=%wide.region_5.6_spmd, body=%wide.region_4.5_spmd.sunk | while | flops 196622 | bytes 655595 | solution.py:32
  208.1 1.0 convert_add_fusion.4
  209.2 1.0 convert_add_fusion.4
  210.2 1.0 convert_add_fusion.4
  211.3 1.0 convert_add_fusion.4
  212.3 1.0 convert_add_fusion.4
  213.4 1.0 convert_add_fusion.4
  214.5 1.0 convert_add_fusion.4
  215.5 1.0 convert_add_fusion.4
  216.6 1.0 convert_add_fusion.4
  217.6 1.0 convert_add_fusion.4
  218.7 1.0 convert_add_fusion.4
  219.8 1.0 convert_add_fusion.4
  220.8 1.0 convert_add_fusion.4
  221.9 1.0 convert_add_fusion.4
  222.9 1.0 convert_add_fusion.4
  224.0 1.0 convert_add_fusion.4
  225.1 1.0 convert_add_fusion.4
  226.1 1.0 convert_add_fusion.4
  227.2 1.0 convert_add_fusion.4
  228.2 1.0 convert_add_fusion.4
  229.3 1.0 convert_add_fusion.4
  230.4 1.0 convert_add_fusion.4
  231.4 1.0 convert_add_fusion.4
  232.5 1.0 convert_add_fusion.4
  233.5 1.0 convert_add_fusion.4
  234.6 1.0 convert_add_fusion.4
  235.7 1.0 convert_add_fusion.4
  236.7 1.0 convert_add_fusion.4
  237.8 1.0 convert_add_fusion.4
  238.8 1.0 convert_add_fusion.4
  239.9 1.0 convert_add_fusion.4
  241.1 0.6 fusion.10
  241.7 0.6 fusion.16
  242.3 3.6 %fusion.55 = f32[256,4096]{1,0:T(8,128)S(1)} fusion(bf16[256,512]{0,1:T(8,128)(2,1)S(1)} %bitcast.147, bf16[4096,512]{1,0:T(8,128)(2,1)} %param.16), kind=kOutput, calls=%fused_computation.88 | convolution fusion | flops 1073741824 | bytes 8650752 | tf_op jit(solution)/shard_map/dot_general | solution.py:187
  246.0 2.7 fusion.1
  248.7 30.0 %reduce-scatter.2.cloned.1.call-done = bf16[512,256]{0,1:T(8,128)(2,1)} async-done(((bf16[4096,256]{0,1:T(8,128)(2,1)}), bf16[512,256]{0,1:T(8,128)(2,1)}) %reduce-scatter.2.cloned.1.call-update) | async-done | bytes 262160 | tf_op jit(solution)/shard_map/reduce_scatter | solution.py:189
  278.8 1.8 convert_bitcast_fusion
  (66 shorter events, 1.1 us)
Async XLA Ops:
  6.5 45.2 %copy-start = (f32[256,128]{1,0:T(8,128)S(1)}, f32[256,128]{1,0:T(8,128)}, u32[]{:S(2)}) copy-start(f32[256,128]{1,0:T(8,128)} %param.19) | copy-start | bytes 393220
  6.5 34.7 %all-gather.7.cloned.1.call-start = ((), (), s32[]{:S(2)}) async-start(), calls=%async_computation.1 | async-start | bytes 2359296 | tf_op jit(solution)/shard_map/all_gather | solution.py:119
  8.4 117.8 %all-gather.11.cloned.1.call-start = ((), (), s32[]{:S(2)}) async-start(), calls=%async_computation.4 | async-start | bytes 4325376 | tf_op jit(solution)/shard_map/all_gather | solution.py:17
  10.2 35.6 %copy-start.2 = (f32[256,128]{1,0:T(8,128)S(1)}, f32[256,128]{1,0:T(8,128)}, u32[]{:S(2)}) copy-start(f32[256,128]{1,0:T(8,128)} %param.18) | copy-start | bytes 393220
  47.1 4.1 %copy-start.5 = (bf16[512,32]{0,1:T(8,128)(2,1)S(1)}, bf16[512,32]{0,1:T(8,128)(2,1)}, u32[]{:S(2)}) copy-start(bf16[512,32]{0,1:T(8,128)(2,1)} %param.22) | copy-start | bytes 98308
  47.1 4.1 %copy-start.6 = (s32[256]{0:T(256)S(1)}, s32[256]{0:T(256)}, u32[]{:S(2)}) copy-start(s32[256]{0:T(256)} %param.23) | copy-start | bytes 3076
  47.1 160.9 %all-gather.9.cloned.1.call-start = ((), (), s32[]{:S(2)}) async-start(), calls=%async_computation.3 | async-start | bytes 4325376 | tf_op jit(solution)/shard_map/all_gather | solution.py:17
  51.2 1.8 copy-start.3
  53.0 225.7 %reduce-scatter.2.cloned.1.call-start = ((), (), s32[]{:S(2)}) async-start(), calls=%async_computation.2 | async-start | bytes 2359296 | tf_op jit(solution)/shard_map/reduce_scatter | solution.py:189
  126.3 0.7 copy-start.4
  242.3 3.7 %copy-start.1 = (bf16[4096,512]{1,0:T(8,128)(2,1)S(1)}, bf16[4096,512]{1,0:T(8,128)(2,1)}, u32[]{:S(2)}) copy-start(bf16[4096,512]{1,0:T(8,128)(2,1)} %param.17) | copy-start | bytes 12582916
Sparse Core Ops, SparseCore 0:
  9.2 32.0 all-gather.6
  47.2 79.0 all-gather.10
  128.8 79.1 all-gather.8
  248.9 29.8 reduce-scatter.1
where the time goes:
time: 290 us; the launch traced here: 287 us
  waiting for transfers between devices  172 us (59%)
  other arithmetic  37.9 us (13%)
  blocking collectives  34.2 us (12%)
  matrix products  26.7 us (9%)
  between operations  13.4 us (5%)
    all_gather x2, waiting for transfers between devices, entering(): lax.all_gather(a.astype(kind), axis)  111 us
    all_gather x1, blocking collectives, entering(): lax.all_gather(a.astype(kind), axis)  34.2 us
    add x31, other arithmetic, backward_combine(): later_part[1] + jnp.exp(later_part[0])[..., None, None] * earlier_part[1]  31.6 us
    all_gather x1, waiting for transfers between devices, local(): shard_piece = lax.all_gather(mixed, 'head', axis=1, tiled=True)  31 us
    reduce_scatter x1, waiting for transfers between devices, local(): lax.psum_scatter((term_x + term_z).astype(jnp.bfloat16), 'head', scatter_...  30 us
  transfers between devices with their start and end apart: 4, of which 4 were waited for; matrix products, arithmetic and copies ran while one was open for 6% of the time, Pallas kernels for 0%

commit v1 on v0

v1 whole, which is shorter than its diff:
```python
import functools

import jax
import jax.numpy as jnp
from jax import lax
from jax.experimental import pallas as pl
from jax.experimental.pallas import tpu as pltpu
from jax.sharding import PartitionSpec as P

F32 = jnp.float32
BF16 = jnp.bfloat16
MESH = pl.DeviceIdType.MESH
NX = 4
PRECISE = lax.Precision.HIGHEST
LO, HI = 0, 1


def dot(a, b):
    return jnp.dot(a, b, preferred_element_type=F32)


def dot_t(a, b, precision=None):
    return lax.dot_general(
        a, b, (((1,), (1,)), ((), ())), preferred_element_type=F32, precision=precision
    )


class Links:
    def __init__(self, send_sems, recv_sems):
        self.send_sems, self.recv_sems = send_sems, recv_sems
        self.sent = []

    def make(self, k, src, dst, device):
        return pltpu.make_async_remote_copy(
            src_ref=src,
            dst_ref=dst,
            send_sem=self.send_sems.at[k],
            recv_sem=self.recv_sems.at[k],
            device_id=device,
            device_id_type=MESH,
        )

    def send(self, k, src, dst, device):
        copy = self.make(k, src, dst, device)
        copy.start()
        self.sent.append(copy)

    def arrive(self, k, dst, device):
        self.make(k, dst, dst, device).wait_recv()

    def finish(self):
        for copy in self.sent:
            copy.wait_send()


def kernel(
    nz,
    ny,
    emb_h,
    noise_h,
    wx_h,
    wz_h,
    b_h,
    c_h,
    ld_h,
    cw_h,
    lab_h,
    skip_s,
    out_h,
    ev,
    nv,
    wx,
    wz,
    bv,
    cv,
    ldv,
    cwv,
    labv,
    mix,
    acc,
    dec_in,
    dec_out,
    cols,
    wts,
    wts_t,
    b_t,
    c_t,
    tots,
    tots_x,
    group,
    groups,
    f_send,
    b_send,
    f_x,
    b_x,
    f_pre,
    b_pre,
    f_tot,
    b_tot,
    t_z,
    f_back,
    b_back,
    f_in,
    b_in,
    y_loc,
    gx_loc,
    fz,
    gx,
    gz,
    s_sib,
    r_sib,
    cs_opp,
    r_lo,
    r_hi,
    cs_r,
    cs_l,
    s_right,
    s_left,
    r_left,
    r_right,
    outv,
    local_sems,
    send_sems,
    recv_sems,
):
    tok, feat = ev.shape
    half = tok // 2
    width = acc.shape[1] // 2
    heads = ldv.shape[0]
    head_dim = width // heads
    state = bv.shape[1]
    lanes = width // NX
    seq, head = lax.axis_index("seq"), lax.axis_index("head")
    z, x = seq // NX, seq % NX
    y, core = head // 2, head % 2
    other = 1 - 2 * core

    links = Links(send_sems, recv_sems)
    counter = [0]

    def new(count=1):
        first = counter[0]
        counter[0] += count
        return first

    pairs = [
        (emb_h, ev),
        (noise_h, nv),
        (ld_h, ldv),
        (b_h, bv),
        (c_h, cv),
        (cw_h, cwv),
        (lab_h, labv),
        (wx_h, wx),
        (wz_h, wz),
    ]
    loads = [pltpu.make_async_copy(s, d, local_sems.at[i]) for i, (s, d) in enumerate(pairs)]
    for load in loads:
        load.start()

    sib = {"head": head + other}
    blk_r = ((y + 1) % ny) * 2 + core
    blk_l = ((y + ny - 1) % ny) * 2 + core
    blk_o = ((y + 2) % ny) * 2 + core
    right, left = {"head": blk_r}, {"head": blk_l}

    def at_x(d):
        return (x + d) % NX

    def at_z(d):
        return (z + d) % nz

    def dev_x(d):
        return {"seq": z * NX + at_x(d)}

    def dev_z(d):
        return {"seq": at_z(d) * NX + x}

    barrier = pltpu.get_barrier_semaphore()
    partners = [sib, right, left]
    partners += [dev_x(d) for d in range(1, NX)] + [dev_z(d) for d in range(1, nz)]
    for partner in partners:
        pl.semaphore_signal(barrier, inc=1, device_id=partner, device_id_type=MESH)

    loads[0].wait()
    loads[1].wait()
    mix[head] = (ev[...].astype(F32) + nv[...].astype(F32)).astype(BF16)
    pl.semaphore_wait(barrier, len(partners))

    part = (pl.ds(0, half), pl.ds(half, half))

    def piece(blk, h):
        return mix.at[blk, part[h]]

    k_r, k_l, k_own = new(2), new(2), new()
    k_fr, k_fl = new(), new()
    k_sib = {name: new(2) for name in ("l", "r", "o")}

    def hand_on(name, blk, h):
        links.send(k_sib[name] + h, piece(blk, h), piece(blk, h), sib)

    def from_sib(name, blk):
        for h in (LO, HI):
            links.arrive(k_sib[name] + h, piece(blk, h), sib)

    links.send(k_r + LO, piece(head, LO), piece(head, LO), right)
    links.send(k_l + HI, piece(head, HI), piece(head, HI), left)
    links.send(k_own, mix.at[head], mix.at[head], sib)
    links.send(k_r + HI, piece(head, HI), piece(head, HI), right)
    links.send(k_l + LO, piece(head, LO), piece(head, LO), left)

    loads[2].wait()
    rates = ldv[...]
    ones_t = lax.broadcasted_iota(jnp.int32, (tok, tok), 0)
    ones_s = lax.broadcasted_iota(jnp.int32, (tok, tok), 1)
    lower = ones_t >= ones_s
    tri = jnp.where(lower, 1.0, 0.0).astype(F32)
    tri_t = jnp.where(ones_s >= ones_t, 1.0, 0.0).astype(F32)
    cum_row = jnp.dot(rates, tri_t, preferred_element_type=F32, precision=PRECISE)
    wide = jnp.concatenate(
        [jnp.broadcast_to(rates[h : h + 1, :], (head_dim, tok)) for h in range(heads)], axis=0
    )
    cum = dot_t(tri, wide, PRECISE)
    total = cum[tok - 1 : tok, :]
    dec_in[...] = jnp.exp(cum)
    dec_out[...] = jnp.exp(total - cum)
    for q in range(NX):
        tots[q] = jnp.broadcast_to(total[:, q * lanes : (q + 1) * lanes], (8, lanes))
    k_tx = new(NX)
    for d in range(1, NX):
        links.send(k_tx + d, tots.at[at_x(d)], tots_x.at[x], dev_x(d))
    tots_x[x] = tots[x]

    loads[3].wait()
    loads[4].wait()
    b_all, c_all = bv[...], cv[...]
    scores = dot_t(c_all, b_all, PRECISE)
    scores_t = dot_t(b_all, c_all, PRECISE)
    b_t[...] = b_all.T.astype(BF16)
    c_t[...] = c_all.T.astype(BF16)

    def span_weights(h):
        down = jnp.broadcast_to(cum[:, h * head_dim : h * head_dim + 1], (tok, tok))
        across = jnp.broadcast_to(cum_row[h : h + 1, :], (tok, tok))
        fall = jnp.exp(jnp.minimum(down - across, 0.0))
        wts[h] = (jnp.where(lower, fall, 0.0) * scores).astype(BF16)
        rise = jnp.exp(jnp.minimum(across - down, 0.0))
        wts_t[h] = (jnp.where(ones_s >= ones_t, rise, 0.0) * scores_t).astype(BF16)

    def project(blk, first=False):
        m = mix[blk]
        for i, w in enumerate((wx, wz)):
            span = slice(i * width, (i + 1) * width)
            term = dot(m, w[blk])
            acc[:, span] = term if first else acc[:, span] + term

    for h in range(0, 2):
        span_weights(h)
    loads[7].wait()
    loads[8].wait()
    project(head, True)

    links.arrive(k_r + LO, piece(blk_l, LO), left)
    links.send(k_fr, piece(blk_l, LO), piece(blk_l, LO), right)
    hand_on("l", blk_l, LO)
    links.arrive(k_l + HI, piece(blk_r, HI), right)
    links.send(k_fl, piece(blk_r, HI), piece(blk_r, HI), left)
    hand_on("r", blk_r, HI)

    for d in range(1, NX):
        links.arrive(k_tx + d, tots_x.at[at_x(NX - d)], dev_x(d))
    group[...] = tots_x[0] + tots_x[1] + tots_x[2] + tots_x[3]
    k_tz = new(nz)
    for d in range(1, nz):
        links.send(k_tz + d, group, groups.at[z], dev_z(d))

    links.arrive(k_own, mix.at[head + other], sib)
    project(head + other)
    for h in range(2, 4):
        span_weights(h)

    links.arrive(k_r + HI, piece(blk_l, HI), left)
    hand_on("l", blk_l, HI)
    links.arrive(k_l + LO, piece(blk_r, LO), right)
    hand_on("r", blk_r, LO)
    for h in range(4, heads):
        span_weights(h)

    loads[5].wait()
    loads[6].wait()
    classes = cwv.shape[1]
    is_label = lax.broadcasted_iota(jnp.int32, (128, tok), 0) == labv[...]
    onehot = jnp.where(is_label, 1.0, 0.0).astype(F32).T[:, :classes].astype(BF16)
    cols[...] = dot_t(onehot, cwv[...])
    for d in range(1, nz):
        links.arrive(k_tz + d, groups.at[at_z(nz - d)], dev_z(d))

    project(blk_l)
    project(blk_r)
    from_sib("l", blk_l + other)
    project(blk_l + other)
    from_sib("r", blk_r + other)
    project(blk_r + other)
    links.arrive(k_fr, piece(blk_o, LO), left)
    hand_on("o", blk_o, LO)
    links.arrive(k_fl, piece(blk_o, HI), right)
    hand_on("o", blk_o, HI)
    project(blk_o)
    from_sib("o", blk_o + other)
    project(blk_o + other)

    def quarter(q):
        return slice(q * lanes, (q + 1) * lanes)

    xs = acc[:, :width]
    x_end = dot(b_t[...], (xs * dec_out[...]).astype(BF16)).astype(BF16)
    for q in range(NX):
        f_send[q] = x_end[:, quarter(q)]
    k_ax = new(NX)
    for d in range(1, NX):
        links.send(k_ax + d, f_send.at[at_x(d)], f_x.at[x], dev_x(d))
    f_x[x] = f_send[x]

    zs = acc[:, width:]
    sig = jax.nn.sigmoid(zs)
    grad_y = cols[...] * (zs * sig)
    g_end = dot(c_t[...], (grad_y * dec_in[...]).astype(BF16)).astype(BF16)
    for q in range(NX):
        b_send[q] = g_end[:, quarter(q)]
    k_ab = new(NX)
    for d in range(1, NX):
        links.send(k_ab + d, b_send.at[at_x(d)], b_x.at[x], dev_x(d))
    b_x[x] = b_send[x]
    fz[...] = cols[...] * sig * (1.0 + zs * (1.0 - sig))

    def fall_of(i):
        return jnp.exp(tots_x[i, 0:1, :])

    for d in range(1, NX):
        links.arrive(k_ax + d, f_x.at[at_x(NX - d)], dev_x(d))
    run = jnp.zeros((state, lanes), F32)
    for i in range(NX):
        f_pre[i] = run
        run = fall_of(i) * run + f_x[i].astype(F32)
    f_tot[...] = run.astype(BF16)
    k_z = new(nz)

    def send_f(d, carry):
        links.make(k_z + d, f_tot, t_z.at[z], {"seq": (z + d) * NX + x}).start()
        return carry

    lax.fori_loop(1, nz - z, send_f, 0)

    for d in range(1, NX):
        links.arrive(k_ab + d, b_x.at[at_x(NX - d)], dev_x(d))
    run = jnp.zeros((state, lanes), F32)
    for i in reversed(range(NX)):
        b_pre[i] = run
        run = fall_of(i) * run + b_x[i].astype(F32)
    b_tot[...] = run.astype(BF16)

    def send_b(d, carry):
        links.make(k_z + d, b_tot, t_z.at[z], {"seq": (z + d - nz) * NX + x}).start()
        return carry

    lax.fori_loop(nz - z, nz, send_b, 0)

    lane = lax.broadcasted_iota(jnp.int32, (tok, lanes), 1)
    first_head = lane < head_dim
    one = lax.broadcasted_iota(jnp.int32, (1, lanes), 1)
    for q in range(NX):
        span = quarter(q)
        gain = jnp.where(one < head_dim, skip_s[2 * q], skip_s[2 * q + 1])
        xq = acc[:, span]
        xb = xq.astype(BF16)
        y_loc[:, span] = (
            jnp.where(first_head, dot(wts[2 * q], xb), dot(wts[2 * q + 1], xb)) + gain * xq
        )
        gq = grad_y[:, span]
        gb = gq.astype(BF16)
        gx_loc[:, span] = (
            jnp.where(first_head, dot(wts_t[2 * q], gb), dot(wts_t[2 * q + 1], gb)) + gain * gq
        )

    def join(i, carry):
        return jnp.exp(groups[i, 0:1, :]) * carry + t_z[i].astype(F32)

    def from_earlier(i, carry):
        links.arrive(k_z + z - i, t_z.at[i], dev_z(1))
        return join(i, carry)

    carry = lax.fori_loop(0, z, from_earlier, jnp.zeros((state, lanes), F32))
    fall = jnp.ones((1, lanes), F32)
    for i in range(NX):
        f_back[i] = (f_pre[i] + fall * carry).astype(BF16)
        fall = fall * fall_of(i)
    k_bf = new(NX)
    for d in range(1, NX):
        links.send(k_bf + d, f_back.at[at_x(d)], f_in.at[x], dev_x(d))
    f_in[x] = f_back[x]

    def from_later(i, carry):
        source = nz - 1 - i
        links.arrive(k_z + nz + z - source, t_z.at[source], dev_z(1))
        return join(source, carry)

    carry = lax.fori_loop(0, nz - 1 - z, from_later, jnp.zeros((state, lanes), F32))
    fall = jnp.ones((1, lanes), F32)
    for i in reversed(range(NX)):
        b_back[i] = (b_pre[i] + fall * carry).astype(BF16)
        fall = fall * fall_of(i)
    k_bb = new(NX)
    for d in range(1, NX):
        links.send(k_bb + d, b_back.at[at_x(d)], b_in.at[x], dev_x(d))
    b_in[x] = b_back[x]

    b_all, c_all = bv[...].astype(BF16), cv[...].astype(BF16)
    for d in range(1, NX):
        links.arrive(k_bf + d, f_in.at[at_x(NX - d)], dev_x(d))
    for q in range(NX):
        span = quarter(q)
        out_y = y_loc[:, span] + dec_in[:, span] * dot(c_all, f_in[q])
        gz[:, span] = (fz[:, span] * out_y).astype(BF16)
    for d in range(1, NX):
        links.arrive(k_bb + d, b_in.at[at_x(NX - d)], dev_x(d))
    for q in range(NX):
        span = quarter(q)
        gx[:, span] = (gx_loc[:, span] + dec_out[:, span] * dot(b_all, b_in[q])).astype(BF16)

    def share(blk):
        return dot_t(gx[...], wx[blk]) + dot_t(gz[...], wz[blk])

    k_rs = new(4)

    def to_sib(slot, blk):
        s_sib[slot] = share(blk + other).astype(BF16)
        links.send(k_rs + slot, s_sib.at[slot], r_sib.at[slot], sib)

    def both(slot, blk):
        mine = share(blk)
        links.arrive(k_rs + slot, r_sib.at[slot], sib)
        return mine + r_sib[slot].astype(F32)

    k_or, k_ol = new(), new()
    k_er, k_el = new(2), new(2)
    lo, hi = part
    to_sib(0, blk_o)
    to_sib(1, blk_r)
    cs_opp[...] = both(0, blk_o).astype(BF16)
    links.send(k_or, cs_opp.at[lo], r_lo, right)
    links.send(k_ol, cs_opp.at[hi], r_hi, left)
    to_sib(2, blk_l)
    cs_r[...] = both(1, blk_r)
    s_right[hi, :] = cs_r[hi, :].astype(BF16)
    links.send(k_er + HI, s_right.at[hi], r_left.at[hi], right)
    cs_l[...] = both(2, blk_l)
    s_left[lo, :] = cs_l[lo, :].astype(BF16)
    links.send(k_el + LO, s_left.at[lo], r_right.at[lo], left)
    to_sib(3, head)
    links.arrive(k_or, r_lo, left)
    s_right[lo, :] = (cs_r[lo, :] + r_lo[...].astype(F32)).astype(BF16)
    links.send(k_er + LO, s_right.at[lo], r_left.at[lo], right)
    links.arrive(k_ol, r_hi, right)
    s_left[hi, :] = (cs_l[hi, :] + r_hi[...].astype(F32)).astype(BF16)
    links.send(k_el + HI, s_left.at[hi], r_right.at[hi], left)
    outv[...] = both(3, head)

    def finish(rows, first, second, i):
        outv[rows, :] = outv[rows, :] + (r_left[rows, :].astype(F32) + r_right[rows, :].astype(F32))
        copy = pltpu.make_async_copy(outv.at[rows], out_h.at[rows], local_sems.at[len(pairs) + i])
        copy.start()
        return copy

    links.arrive(k_el + LO, r_right.at[lo], right)
    links.arrive(k_er + LO, r_left.at[lo], left)
    done_lo = finish(lo, 0, 0, 0)
    links.arrive(k_er + HI, r_left.at[hi], left)
    links.arrive(k_el + HI, r_right.at[hi], right)
    done_hi = finish(hi, 0, 0, 1)

    def sent_f(d, carry):
        links.make(k_z + d, f_tot, f_tot, dev_z(1)).wait_send()
        return carry

    lax.fori_loop(1, nz, sent_f, 0)
    links.finish()
    done_lo.wait()
    done_hi.wait()


SEMS = 96


def local(
    embedding,
    noise_draw,
    weight_x,
    weight_z,
    b_proj,
    c_proj,
    log_decay,
    skip_gain,
    class_weight,
    true_label,
):
    tok, feat = embedding.shape
    width = weight_x.shape[1]
    heads = skip_gain.shape[0]
    state = b_proj.shape[1]
    classes = class_weight.shape[1]
    n_head = lax.axis_size("head")
    nz = lax.axis_size("seq") // NX
    ny = n_head // 2
    lanes = width // NX
    half = tok // 2
    vm = pltpu.VMEM
    quarters = [vm((NX, state, lanes), BF16)] * 2
    scratch = [
        vm((tok, feat), BF16),
        vm((tok, feat), BF16),
        vm((n_head, feat, width), BF16),
        vm((n_head, feat, width), BF16),
        vm((tok, state), F32),
        vm((tok, state), F32),
        vm((heads, tok), F32),
        vm((width, classes), BF16),
        vm((1, tok), jnp.int32),
        vm((n_head, tok, feat), BF16),
        vm((tok, 2 * width), F32),
        vm((tok, width), F32),
        vm((tok, width), F32),
        vm((tok, width), F32),
        vm((heads, tok, tok), BF16),
        vm((heads, tok, tok), BF16),
        vm((state, tok), BF16),
        vm((state, tok), BF16),
        vm((NX, 8, lanes), F32),
        vm((NX, 8, lanes), F32),
        vm((8, lanes), F32),
        vm((nz, 8, lanes), F32),
        *quarters,
        *quarters,
        vm((NX, state, lanes), F32),
        vm((NX, state, lanes), F32),
        vm((state, lanes), BF16),
        vm((state, lanes), BF16),
        vm((nz, state, lanes), BF16),
        *quarters,
        *quarters,
        vm((tok, width), F32),
        vm((tok, width), F32),
        vm((tok, width), F32),
        vm((tok, width), BF16),
        vm((tok, width), BF16),
        vm((4, tok, feat), BF16),
        vm((4, tok, feat), BF16),
        vm((tok, feat), BF16),
        vm((half, feat), BF16),
        vm((half, feat), BF16),
        vm((tok, feat), F32),
        vm((tok, feat), F32),
        vm((tok, feat), BF16),
        vm((tok, feat), BF16),
        vm((tok, feat), BF16),
        vm((tok, feat), BF16),
        vm((tok, feat), F32),
        pltpu.SemaphoreType.DMA((11,)),
        pltpu.SemaphoreType.DMA((SEMS,)),
        pltpu.SemaphoreType.DMA((SEMS,)),
    ]
    anywhere = pl.BlockSpec(memory_space=pl.ANY)
    return pl.pallas_call(
        functools.partial(kernel, nz, ny),
        out_shape=jax.ShapeDtypeStruct((tok, feat), F32),
        in_specs=[anywhere] * 9 + [pl.BlockSpec(memory_space=pltpu.SMEM)],
        out_specs=anywhere,
        scratch_shapes=scratch,
        compiler_params=pltpu.CompilerParams(
            collective_id=0, has_side_effects=True, vmem_limit_bytes=60 * 1024 * 1024
        ),
        cost_estimate=pl.CostEstimate(
            flops=8 * tok * feat * n_head * width,
            bytes_accessed=10 * 1024 * 1024,
            transcendentals=heads * tok * tok * 2,
        ),
    )(
        embedding,
        noise_draw,
        weight_x.reshape(n_head, feat, width),
        weight_z.reshape(n_head, feat, width),
        b_proj,
        c_proj,
        log_decay,
        class_weight,
        true_label.reshape(1, tok),
        skip_gain,
    )


def solution(mesh):
    return jax.shard_map(
        local,
        mesh=mesh,
        in_specs=(
            P("seq", "head"),
            P("seq", "head"),
            P(None, "head"),
            P(None, "head"),
            P("seq", None),
            P("seq", None),
            P("head", "seq"),
            P("head"),
            P("head", None),
            P("seq"),
        ),
        out_specs=P("seq", "head"),
        check_vma=False,
    )
```

time: 290 us -> 60.5 us (0.21)
  waiting for transfers between devices: 172 us -> 0 us
  Pallas kernels: 0 us -> 56.9 us
  other arithmetic: 37.9 us -> 0 us
  blocking collectives: 34.2 us -> 0 us
  matrix products: 26.7 us -> 0 us
  between operations: 13.4 us -> 0.01 us
    all_gather x3 -> x0, waiting for transfers between devices: 142 us -> none  [the longest x2 111 us: entering(): lax.all_gather(a.astype(kind), axis)]
    pallas_call x0 -> x1, Pallas kernels: none -> 56.9 us  [local(): pl.pallas_call(functools.partial(kernel, nz, ny), out_shape=jax.ShapeDtyp...]
    all_gather x1 -> x0, blocking collectives: 34.2 us -> none  [entering(): lax.all_gather(a.astype(kind), axis)]
    add x31 -> x0, other arithmetic: 31.6 us -> none  [backward_combine(): later_part[1] + jnp.exp(later_part[0])[..., None, None] * earlier_part[1]]
    reduce_scatter x1 -> x0, waiting for transfers between devices: 30 us -> none  [local(): lax.psum_scatter((term_x + term_z).astype(jnp.bfloat16), 'head', scatter_...]
    dot_general x14 -> x0, matrix products: 26.7 us -> none  [the longest x1 4.56 us: local(): x_inner = jnp.dot(shard_piece, rows_x, preferred_element_type=jnp.float32)]
    unnamed x14 -> x2, local copies, waits for them, and re-layouts: 0.08 us -> 3.39 us
  transfers between devices with their start and end apart: 4 -> 0, of which waited for: 4 -> 0; matrix products, arithmetic and copies ran while one was open for 6% -> 0% of each run, Pallas kernels for 0% -> 0%
where the time goes in v1:
time: 60.5 us; the launch traced here: 60.3 us
  Pallas kernels  56.9 us (94%)
  local copies, waits for them, and re-layouts  3.39 us (6%)
    pallas_call x1, Pallas kernels, local(): pl.pallas_call(functools.partial(kernel, nz, ny), out_shape=jax.ShapeDtyp...  56.9 us
    unnamed x2, local copies, waits for them, and re-layouts  3.39 us

profile of v1, /device:TPU:1, one launch (start us, length us, event | category | flops | bytes accessed | tf_op | source)
XLA Modules:
  0.0 60.3 jit_solution(13156365382721470449)
XLA Ops:
  0.0 1.5 %copy.11.cw_h = bf16[512,32]{1,0:T(8,128)(2,1)} copy(bf16[512,32]{0,1:T(8,128)(2,1)} %param.18) | data formatting | bytes 65536 | tf_op args[8]
  1.5 56.9 %shard_map.100 = f32[256,512]{1,0:T(8,128)} custom-call(bf16[256,512]{1,0:T(8,128)(2,1)} %emb_h.1, bf16[256,512]{1,0:T(8,128)(2,1)} %noise_h.1, bf16[8,512,512]{2,1,0:T(8,128)(2,1)} %bitcast.3, bf16[8,512,512]{2,1,0:T(8,128)(2,1)} %bitcast.4, f32[256,128]{1,0:T(8,128)} %b_h.1, f32[256,128]{1,0:T(8,128)} %c_h.1, f32[8,256]{1,0:T(8,128)} %ld_h.1, ...), custom_call_target="tpu_custom_call" | custom-call | flops 4294967296 | bytes 10485760 | tf_op jit(solution)/shard_map/pallas_call | solution.py:572
  58.4 1.9 %copy.13 = f32[256,512]{1,0:T(8,128)} copy(f32[256,512]{1,0:T(8,128)} %shard_map.100) | data formatting | bytes 1048576

commit v2 on v1

--- a/solution.py
+++ b/solution.py
@@ -11,6 +11,8 @@
 BF16 = jnp.bfloat16
 MESH = pl.DeviceIdType.MESH
 NX = 4
+NP = 2
+NG = NP * NX
 PRECISE = lax.Precision.HIGHEST
 LO, HI = 0, 1
 
@@ -66,7 +68,7 @@
     cw_h,
     lab_h,
     skip_s,
-    out_h,
+    out,
     ev,
     nv,
     wx,
@@ -86,7 +88,7 @@
     b_t,
     c_t,
     tots,
-    tots_x,
+    tots_m,
     group,
     groups,
     f_send,
@@ -97,7 +99,7 @@
     b_pre,
     f_tot,
     b_tot,
-    t_z,
+    t_g,
     f_back,
     b_back,
     f_in,
@@ -119,6 +121,7 @@
     r_left,
     r_right,
     outv,
+    early,
     local_sems,
     send_sems,
     recv_sems,
@@ -164,21 +167,24 @@
     blk_o = ((y + 2) % ny) * 2 + core
     right, left = {"head": blk_r}, {"head": blk_l}
 
-    def at_x(d):
-        return (x + d) % NX
-
-    def at_z(d):
-        return (z + d) % nz
-
-    def dev_x(d):
-        return {"seq": z * NX + at_x(d)}
-
-    def dev_z(d):
-        return {"seq": at_z(d) * NX + x}
+    ng = nz // NP
+    me, mine = (z % NP) * NX + x, z // NP
+
+    def at_m(d):
+        return (me + d) % NG
+
+    def at_g(d):
+        return (mine + d) % ng
+
+    def dev_m(d):
+        return {"seq": mine * NG + at_m(d)}
+
+    def dev_g(d):
+        return {"seq": at_g(d) * NG + me}
 
     barrier = pltpu.get_barrier_semaphore()
     partners = [sib, right, left]
-    partners += [dev_x(d) for d in range(1, NX)] + [dev_z(d) for d in range(1, nz)]
+    partners += [dev_m(d) for d in range(1, NG)] + [dev_g(d) for d in range(1, ng)]
     for partner in partners:
         pl.semaphore_signal(barrier, inc=1, device_id=partner, device_id_type=MESH)
 
@@ -226,10 +232,24 @@
     dec_out[...] = jnp.exp(total - cum)
     for q in range(NX):
         tots[q] = jnp.broadcast_to(total[:, q * lanes : (q + 1) * lanes], (8, lanes))
-    k_tx = new(NX)
-    for d in range(1, NX):
-        links.send(k_tx + d, tots.at[at_x(d)], tots_x.at[x], dev_x(d))
-    tots_x[x] = tots[x]
+    k_tm = new(NG)
+    for d in range(1, NG):
+        links.send(k_tm + d, tots.at[at_m(d) % NX], tots_m.at[me], dev_m(d))
+    tots_m[me] = tots[x]
+
+    links.arrive(k_r + LO, piece(blk_l, LO), left)
+    links.send(k_fr, piece(blk_l, LO), piece(blk_l, LO), right)
+    hand_on("l", blk_l, LO)
+    links.arrive(k_l + HI, piece(blk_r, HI), right)
+    links.send(k_fl, piece(blk_r, HI), piece(blk_r, HI), left)
+    hand_on("r", blk_r, HI)
+
+    loads[5].wait()
+    loads[6].wait()
+    classes = cwv.shape[0]
+    is_label = lax.broadcasted_iota(jnp.int32, (128, tok), 0) == labv[...]
+    onehot = jnp.where(is_label, 1.0, 0.0).astype(F32).T[:, :classes].astype(BF16)
+    cols[...] = dot(onehot, cwv[...])
 
     loads[3].wait()
     loads[4].wait()
@@ -260,40 +280,19 @@
     loads[8].wait()
     project(head, True)
 
-    links.arrive(k_r + LO, piece(blk_l, LO), left)
-    links.send(k_fr, piece(blk_l, LO), piece(blk_l, LO), right)
-    hand_on("l", blk_l, LO)
-    links.arrive(k_l + HI, piece(blk_r, HI), right)
-    links.send(k_fl, piece(blk_r, HI), piece(blk_r, HI), left)
-    hand_on("r", blk_r, HI)
-
-    for d in range(1, NX):
-        links.arrive(k_tx + d, tots_x.at[at_x(NX - d)], dev_x(d))
-    group[...] = tots_x[0] + tots_x[1] + tots_x[2] + tots_x[3]
-    k_tz = new(nz)
-    for d in range(1, nz):
-        links.send(k_tz + d, group, groups.at[z], dev_z(d))
-
     links.arrive(k_own, mix.at[head + other], sib)
-    project(head + other)
-    for h in range(2, 4):
-        span_weights(h)
-
     links.arrive(k_r + HI, piece(blk_l, HI), left)
     hand_on("l", blk_l, HI)
     links.arrive(k_l + LO, piece(blk_r, LO), right)
     hand_on("r", blk_r, LO)
-    for h in range(4, heads):
-        span_weights(h)
-
-    loads[5].wait()
-    loads[6].wait()
-    classes = cwv.shape[1]
-    is_label = lax.broadcasted_iota(jnp.int32, (128, tok), 0) == labv[...]
-    onehot = jnp.where(is_label, 1.0, 0.0).astype(F32).T[:, :classes].astype(BF16)
-    cols[...] = dot_t(onehot, cwv[...])
-    for d in range(1, nz):
-        links.arrive(k_tz + d, groups.at[at_z(nz - d)], dev_z(d))
+    project(head + other)
+
+    for d in range(1, NG):
+        links.arrive(k_tm + d, tots_m.at[at_m(NG - d)], dev_m(d))
+    group[...] = functools.reduce(lambda a, b: a + b, [tots_m[i] for i in range(NG)])
+    k_tg = new(ng)
+    for d in range(1, ng):
+        links.send(k_tg + d, group, groups.at[mine], dev_g(d))
 
     project(blk_l)
     project(blk_r)
@@ -301,6 +300,9 @@
     project(blk_l + other)
     from_sib("r", blk_r + other)
     project(blk_r + other)
+    for h in range(2, 4):
+        span_weights(h)
+
     links.arrive(k_fr, piece(blk_o, LO), left)
     hand_on("o", blk_o, LO)
     links.arrive(k_fl, piece(blk_o, HI), right)
@@ -314,56 +316,64 @@
 
     xs = acc[:, :width]
     x_end = dot(b_t[...], (xs * dec_out[...]).astype(BF16)).astype(BF16)
-    for q in range(NX):
-        f_send[q] = x_end[:, quarter(q)]
-    k_ax = new(NX)
-    for d in range(1, NX):
-        links.send(k_ax + d, f_send.at[at_x(d)], f_x.at[x], dev_x(d))
-    f_x[x] = f_send[x]
+    rows = state // NP
+    for i in range(NG):
+        f_send[i] = x_end[i // NX * rows : (i // NX + 1) * rows, quarter(i % NX)]
+    k_ax = new(NG)
+    for d in range(1, NG):
+        links.send(k_ax + d, f_send.at[at_m(d)], f_x.at[me], dev_m(d))
+    f_x[me] = f_send[me]
 
     zs = acc[:, width:]
     sig = jax.nn.sigmoid(zs)
     grad_y = cols[...] * (zs * sig)
     g_end = dot(c_t[...], (grad_y * dec_in[...]).astype(BF16)).astype(BF16)
-    for q in range(NX):
-        b_send[q] = g_end[:, quarter(q)]
-    k_ab = new(NX)
-    for d in range(1, NX):
-        links.send(k_ab + d, b_send.at[at_x(d)], b_x.at[x], dev_x(d))
-    b_x[x] = b_send[x]
+    for i in range(NG):
+        b_send[i] = g_end[i // NX * rows : (i // NX + 1) * rows, quarter(i % NX)]
+    k_ab = new(NG)
+    for d in range(1, NG):
+        links.send(k_ab + d, b_send.at[at_m(d)], b_x.at[me], dev_m(d))
+    b_x[me] = b_send[me]
     fz[...] = cols[...] * sig * (1.0 + zs * (1.0 - sig))
+    for h in range(4, heads):
+        span_weights(h)
+    for d in range(1, ng):
+        links.arrive(k_tg + d, groups.at[at_g(ng - d)], dev_g(d))
 
     def fall_of(i):
-        return jnp.exp(tots_x[i, 0:1, :])
-
-    for d in range(1, NX):
-        links.arrive(k_ax + d, f_x.at[at_x(NX - d)], dev_x(d))
-    run = jnp.zeros((state, lanes), F32)
-    for i in range(NX):
+        return jnp.exp(tots_m[i, 0:1, :])
+
+    def nothing():
+        return jnp.zeros((rows, lanes), F32)
+
+    for d in range(1, NG):
+        links.arrive(k_ax + d, f_x.at[at_m(NG - d)], dev_m(d))
+    run = nothing()
+    for i in range(NG):
         f_pre[i] = run
         run = fall_of(i) * run + f_x[i].astype(F32)
     f_tot[...] = run.astype(BF16)
-    k_z = new(nz)
+    k_g = new(ng)
 
     def send_f(d, carry):
-        links.make(k_z + d, f_tot, t_z.at[z], {"seq": (z + d) * NX + x}).start()
+        links.make(k_g + d, f_tot, t_g.at[mine], {"seq": (mine + d) * NG + me}).start()
         return carry
 
-    lax.fori_loop(1, nz - z, send_f, 0)
-
-    for d in range(1, NX):
-        links.arrive(k_ab + d, b_x.at[at_x(NX - d)], dev_x(d))
-    run = jnp.zeros((state, lanes), F32)
-    for i in reversed(range(NX)):
+    lax.fori_loop(1, ng - mine, send_f, 0)
+
+    for d in range(1, NG):
+        links.arrive(k_ab + d, b_x.at[at_m(NG - d)], dev_m(d))
+    run = nothing()
+    for i in reversed(range(NG)):
         b_pre[i] = run
         run = fall_of(i) * run + b_x[i].astype(F32)
     b_tot[...] = run.astype(BF16)
 
     def send_b(d, carry):
-        links.make(k_z + d, b_tot, t_z.at[z], {"seq": (z + d - nz) * NX + x}).start()
+        links.make(k_g + d, b_tot, t_g.at[mine], {"seq": (mine + d - ng) * NG + me}).start()
         return carry
 
-    lax.fori_loop(nz - z, nz, send_b, 0)
+    lax.fori_loop(ng - mine, ng, send_b, 0)
 
     lane = lax.broadcasted_iota(jnp.int32, (tok, lanes), 1)
     first_head = lane < head_dim
@@ -383,70 +393,76 @@
         )
 
     def join(i, carry):
-        return jnp.exp(groups[i, 0:1, :]) * carry + t_z[i].astype(F32)
+        return jnp.exp(groups[i, 0:1, :]) * carry + t_g[i].astype(F32)
 
     def from_earlier(i, carry):
-        links.arrive(k_z + z - i, t_z.at[i], dev_z(1))
+        links.arrive(k_g + mine - i, t_g.at[i], dev_g(1))
         return join(i, carry)
 
-    carry = lax.fori_loop(0, z, from_earlier, jnp.zeros((state, lanes), F32))
+    carry = lax.fori_loop(0, mine, from_earlier, nothing())
     fall = jnp.ones((1, lanes), F32)
-    for i in range(NX):
+    for i in range(NG):
         f_back[i] = (f_pre[i] + fall * carry).astype(BF16)
         fall = fall * fall_of(i)
-    k_bf = new(NX)
-    for d in range(1, NX):
-        links.send(k_bf + d, f_back.at[at_x(d)], f_in.at[x], dev_x(d))
-    f_in[x] = f_back[x]
+    k_bf = new(NG)
+    for d in range(1, NG):
+        links.send(k_bf + d, f_back.at[at_m(d)], f_in.at[me], dev_m(d))
+    f_in[me] = f_back[me]
 
     def from_later(i, carry):
-        source = nz - 1 - i
-        links.arrive(k_z + nz + z - source, t_z.at[source], dev_z(1))
+        source = ng - 1 - i
+        links.arrive(k_g + ng + mine - source, t_g.at[source], dev_g(1))
         return join(source, carry)
 
-    carry = lax.fori_loop(0, nz - 1 - z, from_later, jnp.zeros((state, lanes), F32))
+    carry = lax.fori_loop(0, ng - 1 - mine, from_later, nothing())
     fall = jnp.ones((1, lanes), F32)
-    for i in reversed(range(NX)):
+    for i in reversed(range(NG)):
         b_back[i] = (b_pre[i] + fall * carry).astype(BF16)
         fall = fall * fall_of(i)
-    k_bb = new(NX)
-    for d in range(1, NX):
-        links.send(k_bb + d, b_back.at[at_x(d)], b_in.at[x], dev_x(d))
-    b_in[x] = b_back[x]
+    k_bb = new(NG)
+    for d in range(1, NG):
+        links.send(k_bb + d, b_back.at[at_m(d)], b_in.at[me], dev_m(d))
+    b_in[me] = b_back[me]
+
+    def whole(pieces, q):
+        return jnp.concatenate([pieces[q + p * NX] for p in range(NP)], axis=0)
 
     b_all, c_all = bv[...].astype(BF16), cv[...].astype(BF16)
-    for d in range(1, NX):
-        links.arrive(k_bf + d, f_in.at[at_x(NX - d)], dev_x(d))
+    for d in range(1, NG):
+        links.arrive(k_bf + d, f_in.at[at_m(NG - d)], dev_m(d))
     for q in range(NX):
         span = quarter(q)
-        out_y = y_loc[:, span] + dec_in[:, span] * dot(c_all, f_in[q])
+        out_y = y_loc[:, span] + dec_in[:, span] * dot(c_all, whole(f_in, q))
         gz[:, span] = (fz[:, span] * out_y).astype(BF16)
-    for d in range(1, NX):
-        links.arrive(k_bb + d, b_in.at[at_x(NX - d)], dev_x(d))
+    for i, blk in enumerate((blk_o + other, blk_o)):
+        early[i] = dot_t(gz[...], wz[blk])
+    for d in range(1, NG):
+        links.arrive(k_bb + d, b_in.at[at_m(NG - d)], dev_m(d))
     for q in range(NX):
         span = quarter(q)
-        gx[:, span] = (gx_loc[:, span] + dec_out[:, span] * dot(b_all, b_in[q])).astype(BF16)
-
-    def share(blk):
-        return dot_t(gx[...], wx[blk]) + dot_t(gz[...], wz[blk])
+        gx[:, span] = (gx_loc[:, span] + dec_out[:, span] * dot(b_all, whole(b_in, q))).astype(BF16)
+
+    def share(blk, done=None):
+        from_z = dot_t(gz[...], wz[blk]) if done is None else early[done]
+        return dot_t(gx[...], wx[blk]) + from_z
 
     k_rs = new(4)
 
-    def to_sib(slot, blk):
-        s_sib[slot] = share(blk + other).astype(BF16)
+    def to_sib(slot, blk, done=None):
+        s_sib[slot] = share(blk + other, done).astype(BF16)
         links.send(k_rs + slot, s_sib.at[slot], r_sib.at[slot], sib)
 
-    def both(slot, blk):
-        mine = share(blk)
+    def both(slot, blk, done=None):
+        own = share(blk, done)
         links.arrive(k_rs + slot, r_sib.at[slot], sib)
-        return mine + r_sib[slot].astype(F32)
+        return own + r_sib[slot].astype(F32)
 
     k_or, k_ol = new(), new()
     k_er, k_el = new(2), new(2)
     lo, hi = part
-    to_sib(0, blk_o)
+    to_sib(0, blk_o, 0)
     to_sib(1, blk_r)
-    cs_opp[...] = both(0, blk_o).astype(BF16)
+    cs_opp[...] = both(0, blk_o, 1).astype(BF16)
     links.send(k_or, cs_opp.at[lo], r_lo, right)
     links.send(k_ol, cs_opp.at[hi], r_hi, left)
     to_sib(2, blk_l)
@@ -465,27 +481,22 @@
     links.send(k_el + HI, s_left.at[hi], r_right.at[hi], left)
     outv[...] = both(3, head)
 
-    def finish(rows, first, second, i):
-        outv[rows, :] = outv[rows, :] + (r_left[rows, :].astype(F32) + r_right[rows, :].astype(F32))
-        copy = pltpu.make_async_copy(outv.at[rows], out_h.at[rows], local_sems.at[len(pairs) + i])
-        copy.start()
-        return copy
+    def finish(rows):
+        out[rows, :] = outv[rows, :] + (r_left[rows, :].astype(F32) + r_right[rows, :].astype(F32))
 
     links.arrive(k_el + LO, r_right.at[lo], right)
     links.arrive(k_er + LO, r_left.at[lo], left)
-    done_lo = finish(lo, 0, 0, 0)
+    finish(lo)
     links.arrive(k_er + HI, r_left.at[hi], left)
     links.arrive(k_el + HI, r_right.at[hi], right)
-    done_hi = finish(hi, 0, 0, 1)
+    finish(hi)
 
     def sent_f(d, carry):
-        links.make(k_z + d, f_tot, f_tot, dev_z(1)).wait_send()
+        links.make(k_g + d, f_tot, f_tot, dev_g(1)).wait_send()
         return carry
 
-    lax.fori_loop(1, nz, sent_f, 0)
+    lax.fori_loop(1, ng, sent_f, 0)
     links.finish()
-    done_lo.wait()
-    done_hi.wait()
 
 
 SEMS = 96
@@ -514,7 +525,8 @@
     lanes = width // NX
     half = tok // 2
     vm = pltpu.VMEM
-    quarters = [vm((NX, state, lanes), BF16)] * 2
+    rows = state // NP
+    eighths = [vm((NG, rows, lanes), BF16)] * 2
     scratch = [
         vm((tok, feat), BF16),
         vm((tok, feat), BF16),
@@ -523,7 +535,7 @@
         vm((tok, state), F32),
         vm((tok, state), F32),
         vm((heads, tok), F32),
-        vm((width, classes), BF16),
+        vm((classes, width), BF16),
         vm((1, tok), jnp.int32),
         vm((n_head, tok, feat), BF16),
         vm((tok, 2 * width), F32),
@@ -535,18 +547,18 @@
         vm((state, tok), BF16),
         vm((state, tok), BF16),
         vm((NX, 8, lanes), F32),
-        vm((NX, 8, lanes), F32),
+        vm((NG, 8, lanes), F32),
         vm((8, lanes), F32),
-        vm((nz, 8, lanes), F32),
-        *quarters,
-        *quarters,
-        vm((NX, state, lanes), F32),
-        vm((NX, state, lanes), F32),
-        vm((state, lanes), BF16),
-        vm((state, lanes), BF16),
-        vm((nz, state, lanes), BF16),
-        *quarters,
-        *quarters,
+        vm((nz // NP, 8, lanes), F32),
+        *eighths,
+        *eighths,
+        vm((NG, rows, lanes), F32),
+        vm((NG, rows, lanes), F32),
+        vm((rows, lanes), BF16),
+        vm((rows, lanes), BF16),
+        vm((nz // NP, rows, lanes), BF16),
+        *eighths,
+        *eighths,
         vm((tok, width), F32),
         vm((tok, width), F32),
         vm((tok, width), F32),
@@ -564,16 +576,17 @@
         vm((tok, feat), BF16),
         vm((tok, feat), BF16),
         vm((tok, feat), F32),
-        pltpu.SemaphoreType.DMA((11,)),
+        vm((2, tok, feat), F32),
+        pltpu.SemaphoreType.DMA((9,)),
         pltpu.SemaphoreType.DMA((SEMS,)),
         pltpu.SemaphoreType.DMA((SEMS,)),
     ]
     anywhere = pl.BlockSpec(memory_space=pl.ANY)
     return pl.pallas_call(
         functools.partial(kernel, nz, ny),
-        out_shape=jax.ShapeDtypeStruct((tok, feat), F32),
+        out_shape=pltpu.VMEM((tok, feat), F32),
         in_specs=[anywhere] * 9 + [pl.BlockSpec(memory_space=pltpu.SMEM)],
-        out_specs=anywhere,
+        out_specs=pl.BlockSpec(memory_space=pltpu.VMEM),
         scratch_shapes=scratch,
         compiler_params=pltpu.CompilerParams(
             collective_id=0, has_side_effects=True, vmem_limit_bytes=60 * 1024 * 1024
@@ -591,7 +604,7 @@
         b_proj,
         c_proj,
         log_decay,
-        class_weight,
+        class_weight.T,
         true_label.reshape(1, tok),
         skip_gain,
     )

time: 60.5 us -> 53.3 us (0.88)
  Pallas kernels: 56.9 us -> 52.4 us
  local copies, waits for them, and re-layouts: 3.39 us -> 0.8 us
    pallas_call x1, Pallas kernels: 56.9 us -> 52.4 us  [local(): pl.pallas_call(functools.partial(kernel, nz, ny), out_shape=pltpu.VMEM((t...]
    unnamed x2 -> x1, local copies, waits for them, and re-layouts: 3.39 us -> 0.8 us
where the time goes in v2:
time: 53.3 us; the launch traced here: 53.2 us
  Pallas kernels  52.4 us (98%)
  local copies, waits for them, and re-layouts  0.8 us (2%)
    pallas_call x1, Pallas kernels, local(): pl.pallas_call(functools.partial(kernel, nz, ny), out_shape=pltpu.VMEM((t...  52.4 us

profile of v2, /device:TPU:1, one launch (start us, length us, event | category | flops | bytes accessed | tf_op | source)
XLA Modules:
  0.0 53.2 jit_solution(16393023686122378827)
XLA Ops:
  0.0 52.4 %shard_map.100 = f32[256,512]{1,0:T(8,128)S(1)} custom-call(bf16[256,512]{1,0:T(8,128)(2,1)} %emb_h.1, bf16[256,512]{1,0:T(8,128)(2,1)} %noise_h.1, bf16[8,512,512]{2,1,0:T(8,128)(2,1)} %bitcast.4, bf16[8,512,512]{2,1,0:T(8,128)(2,1)} %bitcast.5, f32[256,128]{1,0:T(8,128)} %b_h.1, f32[256,128]{1,0:T(8,128)} %c_h.1, f32[8,256]{1,0:T(8,128)} %ld_h.1, ...), custom_call_target="tpu_custom_call" | custom-call | flops 4294967296 | bytes 10485760 | tf_op jit(solution)/shard_map/pallas_call | solution.py:585
  52.4 0.8 %copy.12 = f32[256,512]{1,0:T(8,128)} copy(f32[256,512]{1,0:T(8,128)S(1)} %shard_map.100) | data formatting | bytes 1048576

commit v3 on v2

--- a/solution.py
+++ b/solution.py
@@ -15,6 +15,7 @@
 NG = NP * NX
 PRECISE = lax.Precision.HIGHEST
 LO, HI = 0, 1
+HALVES = (LO, HI)
 
 
 def dot(a, b):
@@ -112,8 +113,7 @@
     s_sib,
     r_sib,
     cs_opp,
-    r_lo,
-    r_hi,
+    r_opp,
     cs_r,
     cs_l,
     s_right,
@@ -123,11 +123,12 @@
     outv,
     early,
     local_sems,
+    relay,
     send_sems,
     recv_sems,
 ):
     tok, feat = ev.shape
-    half = tok // 2
+    half = feat // 2
     width = acc.shape[1] // 2
     heads = ldv.shape[0]
     head_dim = width // heads
@@ -183,20 +184,28 @@
         return {"seq": at_g(d) * NG + me}
 
     barrier = pltpu.get_barrier_semaphore()
-    partners = [sib, right, left]
-    partners += [dev_m(d) for d in range(1, NG)] + [dev_g(d) for d in range(1, ng)]
+    near = [{"seq": z * NX + (x + d) % NX} for d in (1, NX - 1)]
+    near += [{"seq": (z + d) % nz * NX + x} for d in (1, nz - 1)]
+    partners = [sib, right, left] + near
     for partner in partners:
         pl.semaphore_signal(barrier, inc=1, device_id=partner, device_id_type=MESH)
 
+    def tell(r):
+        for partner in near:
+            pl.semaphore_signal(relay.at[r], inc=1, device_id=partner, device_id_type=MESH)
+
+    def told(r):
+        pl.semaphore_wait(relay.at[r], len(near))
+
     loads[0].wait()
     loads[1].wait()
-    mix[head] = (ev[...].astype(F32) + nv[...].astype(F32)).astype(BF16)
+    noisy = (ev[...].astype(F32) + nv[...].astype(F32)).astype(BF16)
+    for h in HALVES:
+        mix[head, h] = noisy[:, h * half : (h + 1) * half]
     pl.semaphore_wait(barrier, len(partners))
 
-    part = (pl.ds(0, half), pl.ds(half, half))
-
     def piece(blk, h):
-        return mix.at[blk, part[h]]
+        return mix.at[blk, h]
 
     k_r, k_l, k_own = new(2), new(2), new()
     k_fr, k_fl = new(), new()
@@ -205,15 +214,15 @@
     def hand_on(name, blk, h):
         links.send(k_sib[name] + h, piece(blk, h), piece(blk, h), sib)
 
-    def from_sib(name, blk):
-        for h in (LO, HI):
-            links.arrive(k_sib[name] + h, piece(blk, h), sib)
+    def from_sib(name, blk, h):
+        links.arrive(k_sib[name] + h, piece(blk, h), sib)
 
     links.send(k_r + LO, piece(head, LO), piece(head, LO), right)
     links.send(k_l + HI, piece(head, HI), piece(head, HI), left)
     links.send(k_own, mix.at[head], mix.at[head], sib)
     links.send(k_r + HI, piece(head, HI), piece(head, HI), right)
     links.send(k_l + LO, piece(head, LO), piece(head, LO), left)
+    tell(0)
 
     loads[2].wait()
     rates = ldv[...]
@@ -232,10 +241,9 @@
     dec_out[...] = jnp.exp(total - cum)
     for q in range(NX):
         tots[q] = jnp.broadcast_to(total[:, q * lanes : (q + 1) * lanes], (8, lanes))
-    k_tm = new(NG)
-    for d in range(1, NG):
-        links.send(k_tm + d, tots.at[at_m(d) % NX], tots_m.at[me], dev_m(d))
     tots_m[me] = tots[x]
+    told(0)
+    tell(1)
 
     links.arrive(k_r + LO, piece(blk_l, LO), left)
     links.send(k_fr, piece(blk_l, LO), piece(blk_l, LO), right)
@@ -243,6 +251,11 @@
     links.arrive(k_l + HI, piece(blk_r, HI), right)
     links.send(k_fl, piece(blk_r, HI), piece(blk_r, HI), left)
     hand_on("r", blk_r, HI)
+    told(1)
+    tell(2)
+    k_tm = new(NG)
+    for d in range(1, NG):
+        links.send(k_tm + d, tots.at[at_m(d) % NX], tots_m.at[me], dev_m(d))
 
     loads[5].wait()
     loads[6].wait()
@@ -267,49 +280,54 @@
         rise = jnp.exp(jnp.minimum(across - down, 0.0))
         wts_t[h] = (jnp.where(ones_s >= ones_t, rise, 0.0) * scores_t).astype(BF16)
 
-    def project(blk, first=False):
-        m = mix[blk]
+    def project(blk, h, first=False):
+        m = mix[blk, h]
         for i, w in enumerate((wx, wz)):
             span = slice(i * width, (i + 1) * width)
-            term = dot(m, w[blk])
+            term = dot(m, w[blk, h * half : (h + 1) * half, :])
             acc[:, span] = term if first else acc[:, span] + term
 
     for h in range(0, 2):
         span_weights(h)
     loads[7].wait()
     loads[8].wait()
-    project(head, True)
+    project(head, LO, True)
+    project(head, HI)
 
     links.arrive(k_own, mix.at[head + other], sib)
     links.arrive(k_r + HI, piece(blk_l, HI), left)
     hand_on("l", blk_l, HI)
     links.arrive(k_l + LO, piece(blk_r, LO), right)
     hand_on("r", blk_r, LO)
-    project(head + other)
+    for h in HALVES:
+        project(head + other, h)
 
     for d in range(1, NG):
         links.arrive(k_tm + d, tots_m.at[at_m(NG - d)], dev_m(d))
     group[...] = functools.reduce(lambda a, b: a + b, [tots_m[i] for i in range(NG)])
+    told(2)
     k_tg = new(ng)
     for d in range(1, ng):
         links.send(k_tg + d, group, groups.at[mine], dev_g(d))
 
-    project(blk_l)
-    project(blk_r)
-    from_sib("l", blk_l + other)
-    project(blk_l + other)
-    from_sib("r", blk_r + other)
-    project(blk_r + other)
-    for h in range(2, 4):
-        span_weights(h)
+    for h in HALVES:
+        project(blk_l, h)
+        project(blk_r, h)
+    for h in HALVES:
+        from_sib("l", blk_l + other, h)
+        project(blk_l + other, h)
+        from_sib("r", blk_r + other, h)
+        project(blk_r + other, h)
 
     links.arrive(k_fr, piece(blk_o, LO), left)
     hand_on("o", blk_o, LO)
     links.arrive(k_fl, piece(blk_o, HI), right)
     hand_on("o", blk_o, HI)
-    project(blk_o)
-    from_sib("o", blk_o + other)
-    project(blk_o + other)
+    for h in HALVES:
+        project(blk_o, h)
+    for h in HALVES:
+        from_sib("o", blk_o + other, h)
+        project(blk_o + other, h)
 
     def quarter(q):
         return slice(q * lanes, (q + 1) * lanes)
@@ -335,7 +353,7 @@
         links.send(k_ab + d, b_send.at[at_m(d)], b_x.at[me], dev_m(d))
     b_x[me] = b_send[me]
     fz[...] = cols[...] * sig * (1.0 + zs * (1.0 - sig))
-    for h in range(4, heads):
+    for h in range(2, heads):
         span_weights(h)
     for d in range(1, ng):
         links.arrive(k_tg + d, groups.at[at_g(ng - d)], dev_g(d))
@@ -435,61 +453,66 @@
         out_y = y_loc[:, span] + dec_in[:, span] * dot(c_all, whole(f_in, q))
         gz[:, span] = (fz[:, span] * out_y).astype(BF16)
     for i, blk in enumerate((blk_o + other, blk_o)):
-        early[i] = dot_t(gz[...], wz[blk])
+        for h in HALVES:
+            early[2 * i + h] = dot_t(gz[...], wz[blk, h * half : (h + 1) * half, :])
     for d in range(1, NG):
         links.arrive(k_bb + d, b_in.at[at_m(NG - d)], dev_m(d))
     for q in range(NX):
         span = quarter(q)
         gx[:, span] = (gx_loc[:, span] + dec_out[:, span] * dot(b_all, whole(b_in, q))).astype(BF16)
 
-    def share(blk, done=None):
-        from_z = dot_t(gz[...], wz[blk]) if done is None else early[done]
-        return dot_t(gx[...], wx[blk]) + from_z
-
-    k_rs = new(4)
-
-    def to_sib(slot, blk, done=None):
-        s_sib[slot] = share(blk + other, done).astype(BF16)
-        links.send(k_rs + slot, s_sib.at[slot], r_sib.at[slot], sib)
-
-    def both(slot, blk, done=None):
-        own = share(blk, done)
-        links.arrive(k_rs + slot, r_sib.at[slot], sib)
-        return own + r_sib[slot].astype(F32)
+    def share(blk, h, done):
+        span = slice(h * half, (h + 1) * half)
+        from_z = dot_t(gz[...], wz[blk, span, :]) if done is None else early[done + h]
+        return dot_t(gx[...], wx[blk, span, :]) + from_z
+
+    k_rs = new(8)
+
+    def to_sib(slot, blk, h, done=None):
+        s_sib[slot, h] = share(blk + other, h, done).astype(BF16)
+        links.send(k_rs + 2 * slot + h, s_sib.at[slot, h], r_sib.at[slot, h], sib)
+
+    def both(slot, blk, h, done=None):
+        own = share(blk, h, done)
+        links.arrive(k_rs + 2 * slot + h, r_sib.at[slot, h], sib)
+        return own + r_sib[slot, h].astype(F32)
 
     k_or, k_ol = new(), new()
     k_er, k_el = new(2), new(2)
-    lo, hi = part
-    to_sib(0, blk_o, 0)
-    to_sib(1, blk_r)
-    cs_opp[...] = both(0, blk_o, 1).astype(BF16)
-    links.send(k_or, cs_opp.at[lo], r_lo, right)
-    links.send(k_ol, cs_opp.at[hi], r_hi, left)
-    to_sib(2, blk_l)
-    cs_r[...] = both(1, blk_r)
-    s_right[hi, :] = cs_r[hi, :].astype(BF16)
-    links.send(k_er + HI, s_right.at[hi], r_left.at[hi], right)
-    cs_l[...] = both(2, blk_l)
-    s_left[lo, :] = cs_l[lo, :].astype(BF16)
-    links.send(k_el + LO, s_left.at[lo], r_right.at[lo], left)
-    to_sib(3, head)
-    links.arrive(k_or, r_lo, left)
-    s_right[lo, :] = (cs_r[lo, :] + r_lo[...].astype(F32)).astype(BF16)
-    links.send(k_er + LO, s_right.at[lo], r_left.at[lo], right)
-    links.arrive(k_ol, r_hi, right)
-    s_left[hi, :] = (cs_l[hi, :] + r_hi[...].astype(F32)).astype(BF16)
-    links.send(k_el + HI, s_left.at[hi], r_right.at[hi], left)
-    outv[...] = both(3, head)
-
-    def finish(rows):
-        out[rows, :] = outv[rows, :] + (r_left[rows, :].astype(F32) + r_right[rows, :].astype(F32))
-
-    links.arrive(k_el + LO, r_right.at[lo], right)
-    links.arrive(k_er + LO, r_left.at[lo], left)
-    finish(lo)
-    links.arrive(k_er + HI, r_left.at[hi], left)
-    links.arrive(k_el + HI, r_right.at[hi], right)
-    finish(hi)
+    to_sib(0, blk_o, LO, 0)
+    to_sib(0, blk_o, HI, 0)
+    to_sib(1, blk_r, HI)
+    to_sib(2, blk_l, LO)
+    cs_opp[LO] = both(0, blk_o, LO, 2).astype(BF16)
+    links.send(k_or, cs_opp.at[LO], r_opp.at[LO], right)
+    cs_opp[HI] = both(0, blk_o, HI, 2).astype(BF16)
+    links.send(k_ol, cs_opp.at[HI], r_opp.at[HI], left)
+    s_right[HI] = both(1, blk_r, HI).astype(BF16)
+    links.send(k_er + HI, s_right.at[HI], r_left.at[HI], right)
+    s_left[LO] = both(2, blk_l, LO).astype(BF16)
+    links.send(k_el + LO, s_left.at[LO], r_right.at[LO], left)
+    to_sib(1, blk_r, LO)
+    to_sib(2, blk_l, HI)
+    for h in HALVES:
+        to_sib(3, head, h)
+    cs_r[...] = both(1, blk_r, LO)
+    cs_l[...] = both(2, blk_l, HI)
+    links.arrive(k_or, r_opp.at[LO], left)
+    s_right[LO] = (cs_r[...] + r_opp[LO].astype(F32)).astype(BF16)
+    links.send(k_er + LO, s_right.at[LO], r_left.at[LO], right)
+    links.arrive(k_ol, r_opp.at[HI], right)
+    s_left[HI] = (cs_l[...] + r_opp[HI].astype(F32)).astype(BF16)
+    links.send(k_el + HI, s_left.at[HI], r_right.at[HI], left)
+    for h in HALVES:
+        outv[h] = both(3, head, h)
+    links.arrive(k_el + LO, r_right.at[LO], right)
+    outv[LO] = outv[LO] + r_right[LO].astype(F32)
+    links.arrive(k_er + HI, r_left.at[HI], left)
+    outv[HI] = outv[HI] + r_left[HI].astype(F32)
+    links.arrive(k_er + LO, r_left.at[LO], left)
+    out[:, :half] = outv[LO] + r_left[LO].astype(F32)
+    links.arrive(k_el + HI, r_right.at[HI], right)
+    out[:, half:] = outv[HI] + r_right[HI].astype(F32)
 
     def sent_f(d, carry):
         links.make(k_g + d, f_tot, f_tot, dev_g(1)).wait_send()
@@ -523,8 +546,9 @@
     nz = lax.axis_size("seq") // NX
     ny = n_head // 2
     lanes = width // NX
-    half = tok // 2
+    half = feat // 2
     vm = pltpu.VMEM
+    halves = [vm((2, tok, half), BF16)] * 2
     rows = state // NP
     eighths = [vm((NG, rows, lanes), BF16)] * 2
     scratch = [
@@ -537,7 +561,7 @@
         vm((heads, tok), F32),
         vm((classes, width), BF16),
         vm((1, tok), jnp.int32),
-        vm((n_head, tok, feat), BF16),
+        vm((n_head, 2, tok, half), BF16),
         vm((tok, 2 * width), F32),
         vm((tok, width), F32),
         vm((tok, width), F32),
@@ -564,20 +588,17 @@
         vm((tok, width), F32),
         vm((tok, width), BF16),
         vm((tok, width), BF16),
-        vm((4, tok, feat), BF16),
-        vm((4, tok, feat), BF16),
-        vm((tok, feat), BF16),
-        vm((half, feat), BF16),
-        vm((half, feat), BF16),
-        vm((tok, feat), F32),
-        vm((tok, feat), F32),
-        vm((tok, feat), BF16),
-        vm((tok, feat), BF16),
-        vm((tok, feat), BF16),
-        vm((tok, feat), BF16),
-        vm((tok, feat), F32),
-        vm((2, tok, feat), F32),
+        vm((4, 2, tok, half), BF16),
+        vm((4, 2, tok, half), BF16),
+        *halves,
+        vm((tok, half), F32),
+        vm((tok, half), F32),
+        *halves,
+        *halves,
+        vm((2, tok, half), F32),
+        vm((4, tok, half), F32),
         pltpu.SemaphoreType.DMA((9,)),
+        pltpu.SemaphoreType.REGULAR((3,)),
         pltpu.SemaphoreType.DMA((SEMS,)),
         pltpu.SemaphoreType.DMA((SEMS,)),
     ]

time: 53.3 us -> 52 us (0.976)
  Pallas kernels: 52.4 us -> 51.2 us
    pallas_call x1, Pallas kernels: 52.4 us -> 51.2 us  [local(): pl.pallas_call(functools.partial(kernel, nz, ny), out_shape=pltpu.VMEM((t...]
where the time goes in v3:
time: 52 us
  Pallas kernels  51.2 us (98%)
  local copies, waits for them, and re-layouts  0.8 us (2%)
    pallas_call x1, Pallas kernels, local(): pl.pallas_call(functools.partial(kernel, nz, ny), out_shape=pltpu.VMEM((t...  51.2 us

profile of v3, /device:TPU:1, one launch (start us, length us, event | category | flops | bytes accessed | tf_op | source)
XLA Modules:
  0.0 52.0 jit_solution(3878432991852403988)
XLA Ops:
  0.0 51.2 %shard_map.100 = f32[256,512]{1,0:T(8,128)S(1)} custom-call(bf16[256,512]{1,0:T(8,128)(2,1)} %emb_h.1, bf16[256,512]{1,0:T(8,128)(2,1)} %noise_h.1, bf16[8,512,512]{2,1,0:T(8,128)(2,1)} %bitcast.4, bf16[8,512,512]{2,1,0:T(8,128)(2,1)} %bitcast.5, f32[256,128]{1,0:T(8,128)} %b_h.1, f32[256,128]{1,0:T(8,128)} %c_h.1, f32[8,256]{1,0:T(8,128)} %ld_h.1, ...), custom_call_target="tpu_custom_call" | custom-call | flops 4294967296 | bytes 10485760 | tf_op jit(solution)/shard_map/pallas_call | solution.py:606
  51.2 0.8 %copy.12 = f32[256,512]{1,0:T(8,128)} copy(f32[256,512]{1,0:T(8,128)S(1)} %shard_map.100) | data formatting | bytes 1048576

commit v4 on v3

--- a/solution.py
+++ b/solution.py
@@ -68,7 +68,7 @@
     ld_h,
     cw_h,
     lab_h,
-    skip_s,
+    skip_h,
     out,
     ev,
     nv,
@@ -79,6 +79,7 @@
     ldv,
     cwv,
     labv,
+    skipv,
     mix,
     acc,
     dec_in,
@@ -155,6 +156,7 @@
         (c_h, cv),
         (cw_h, cwv),
         (lab_h, labv),
+        (skip_h, skipv),
         (wx_h, wx),
         (wz_h, wz),
     ]
@@ -289,8 +291,8 @@
 
     for h in range(0, 2):
         span_weights(h)
-    loads[7].wait()
     loads[8].wait()
+    loads[9].wait()
     project(head, LO, True)
     project(head, HI)
 
@@ -301,14 +303,6 @@
     hand_on("r", blk_r, LO)
     for h in HALVES:
         project(head + other, h)
-
-    for d in range(1, NG):
-        links.arrive(k_tm + d, tots_m.at[at_m(NG - d)], dev_m(d))
-    group[...] = functools.reduce(lambda a, b: a + b, [tots_m[i] for i in range(NG)])
-    told(2)
-    k_tg = new(ng)
-    for d in range(1, ng):
-        links.send(k_tg + d, group, groups.at[mine], dev_g(d))
 
     for h in HALVES:
         project(blk_l, h)
@@ -353,10 +347,15 @@
         links.send(k_ab + d, b_send.at[at_m(d)], b_x.at[me], dev_m(d))
     b_x[me] = b_send[me]
     fz[...] = cols[...] * sig * (1.0 + zs * (1.0 - sig))
+    for d in range(1, NG):
+        links.arrive(k_tm + d, tots_m.at[at_m(NG - d)], dev_m(d))
+    group[...] = functools.reduce(lambda a, b: a + b, [tots_m[i] for i in range(NG)])
+    told(2)
+    k_tg = new(ng)
+    for d in range(1, ng):
+        links.send(k_tg + d, group, groups.at[mine], dev_g(d))
     for h in range(2, heads):
         span_weights(h)
-    for d in range(1, ng):
-        links.arrive(k_tg + d, groups.at[at_g(ng - d)], dev_g(d))
 
     def fall_of(i):
         return jnp.exp(tots_m[i, 0:1, :])
@@ -396,9 +395,11 @@
     lane = lax.broadcasted_iota(jnp.int32, (tok, lanes), 1)
     first_head = lane < head_dim
     one = lax.broadcasted_iota(jnp.int32, (1, lanes), 1)
+    loads[7].wait()
+    gains = skipv[...]
     for q in range(NX):
         span = quarter(q)
-        gain = jnp.where(one < head_dim, skip_s[2 * q], skip_s[2 * q + 1])
+        gain = jnp.where(one < head_dim, gains[:, 2 * q : 2 * q + 1], gains[:, 2 * q + 1 : 2 * q + 2])
         xq = acc[:, span]
         xb = xq.astype(BF16)
         y_loc[:, span] = (
@@ -409,6 +410,9 @@
         gx_loc[:, span] = (
             jnp.where(first_head, dot(wts_t[2 * q], gb), dot(wts_t[2 * q + 1], gb)) + gain * gq
         )
+
+    for d in range(1, ng):
+        links.arrive(k_tg + d, groups.at[at_g(ng - d)], dev_g(d))
 
     def join(i, carry):
         return jnp.exp(groups[i, 0:1, :]) * carry + t_g[i].astype(F32)
@@ -561,6 +565,7 @@
         vm((heads, tok), F32),
         vm((classes, width), BF16),
         vm((1, tok), jnp.int32),
+        vm((1, heads), F32),
         vm((n_head, 2, tok, half), BF16),
         vm((tok, 2 * width), F32),
         vm((tok, width), F32),
@@ -597,7 +602,7 @@
         *halves,
         vm((2, tok, half), F32),
         vm((4, tok, half), F32),
-        pltpu.SemaphoreType.DMA((9,)),
+        pltpu.SemaphoreType.DMA((10,)),
         pltpu.SemaphoreType.REGULAR((3,)),
         pltpu.SemaphoreType.DMA((SEMS,)),
         pltpu.SemaphoreType.DMA((SEMS,)),
@@ -606,7 +611,7 @@
     return pl.pallas_call(
         functools.partial(kernel, nz, ny),
         out_shape=pltpu.VMEM((tok, feat), F32),
-        in_specs=[anywhere] * 9 + [pl.BlockSpec(memory_space=pltpu.SMEM)],
+        in_specs=[anywhere] * 10,
         out_specs=pl.BlockSpec(memory_space=pltpu.VMEM),
         scratch_shapes=scratch,
         compiler_params=pltpu.CompilerParams(
@@ -627,7 +632,7 @@
         log_decay,
         class_weight.T,
         true_label.reshape(1, tok),
-        skip_gain,
+        skip_gain.reshape(1, heads),
     )
 
 

time: 52 us -> 51 us (0.981)
  Pallas kernels: 51.2 us -> 50.2 us
    pallas_call x1, Pallas kernels: 51.2 us -> 50.2 us  [local(): pl.pallas_call(functools.partial(kernel, nz, ny), out_shape=pltpu.VMEM((t...]
where the time goes in v4:
time: 51 us
  Pallas kernels  50.2 us (98%)
  local copies, waits for them, and re-layouts  0.8 us (2%)
    pallas_call x1, Pallas kernels, local(): pl.pallas_call(functools.partial(kernel, nz, ny), out_shape=pltpu.VMEM((t...  50.2 us

profile of v4, /device:TPU:1, one launch (start us, length us, event | category | flops | bytes accessed | tf_op | source)
XLA Modules:
  0.0 51.0 jit_solution(1379532048223658112)
XLA Ops:
  0.0 50.2 %shard_map.100 = f32[256,512]{1,0:T(8,128)S(1)} custom-call(bf16[256,512]{1,0:T(8,128)(2,1)} %emb_h.1, bf16[256,512]{1,0:T(8,128)(2,1)} %noise_h.1, bf16[8,512,512]{2,1,0:T(8,128)(2,1)} %bitcast.5, bf16[8,512,512]{2,1,0:T(8,128)(2,1)} %bitcast.6, f32[256,128]{1,0:T(8,128)} %b_h.1, f32[256,128]{1,0:T(8,128)} %c_h.1, f32[8,256]{1,0:T(8,128)} %ld_h.1, ...), custom_call_target="tpu_custom_call" | custom-call | flops 4294967296 | bytes 10485760 | tf_op jit(solution)/shard_map/pallas_call | solution.py:611
  50.2 0.8 %copy.12 = f32[256,512]{1,0:T(8,128)} copy(f32[256,512]{1,0:T(8,128)S(1)} %shard_map.100) | data formatting | bytes 1048576

commit v5 on v4

--- a/solution.py
+++ b/solution.py
@@ -452,18 +452,16 @@
     b_all, c_all = bv[...].astype(BF16), cv[...].astype(BF16)
     for d in range(1, NG):
         links.arrive(k_bf + d, f_in.at[at_m(NG - d)], dev_m(d))
-    for q in range(NX):
-        span = quarter(q)
-        out_y = y_loc[:, span] + dec_in[:, span] * dot(c_all, whole(f_in, q))
-        gz[:, span] = (fz[:, span] * out_y).astype(BF16)
+    entered = jnp.concatenate([whole(f_in, q) for q in range(NX)], axis=1)
+    out_y = y_loc[...] + dec_in[...] * dot(c_all, entered)
+    gz[...] = (fz[...] * out_y).astype(BF16)
     for i, blk in enumerate((blk_o + other, blk_o)):
         for h in HALVES:
             early[2 * i + h] = dot_t(gz[...], wz[blk, h * half : (h + 1) * half, :])
     for d in range(1, NG):
         links.arrive(k_bb + d, b_in.at[at_m(NG - d)], dev_m(d))
-    for q in range(NX):
-        span = quarter(q)
-        gx[:, span] = (gx_loc[:, span] + dec_out[:, span] * dot(b_all, whole(b_in, q))).astype(BF16)
+    entered = jnp.concatenate([whole(b_in, q) for q in range(NX)], axis=1)
+    gx[...] = (gx_loc[...] + dec_out[...] * dot(b_all, entered)).astype(BF16)
 
     def share(blk, h, done):
         span = slice(h * half, (h + 1) * half)
@@ -481,42 +479,47 @@
         links.arrive(k_rs + 2 * slot + h, r_sib.at[slot, h], sib)
         return own + r_sib[slot, h].astype(F32)
 
-    k_or, k_ol = new(), new()
-    k_er, k_el = new(2), new(2)
+    k_or, k_ol = new(2), new(2)
+    k_er, k_el = new(3), new(3)
+    parts = [pl.ds(i * (tok // 2), tok // 2) for i in range(2)]
     to_sib(0, blk_o, LO, 0)
     to_sib(0, blk_o, HI, 0)
     to_sib(1, blk_r, HI)
     to_sib(2, blk_l, LO)
     cs_opp[LO] = both(0, blk_o, LO, 2).astype(BF16)
-    links.send(k_or, cs_opp.at[LO], r_opp.at[LO], right)
+    for i, rows in enumerate(parts):
+        links.send(k_or + i, cs_opp.at[LO, rows], r_opp.at[LO, rows], right)
     cs_opp[HI] = both(0, blk_o, HI, 2).astype(BF16)
-    links.send(k_ol, cs_opp.at[HI], r_opp.at[HI], left)
+    for i, rows in enumerate(parts):
+        links.send(k_ol + i, cs_opp.at[HI, rows], r_opp.at[HI, rows], left)
     s_right[HI] = both(1, blk_r, HI).astype(BF16)
-    links.send(k_er + HI, s_right.at[HI], r_left.at[HI], right)
+    links.send(k_er + 2, s_right.at[HI], r_left.at[HI], right)
     s_left[LO] = both(2, blk_l, LO).astype(BF16)
-    links.send(k_el + LO, s_left.at[LO], r_right.at[LO], left)
+    links.send(k_el + 2, s_left.at[LO], r_right.at[LO], left)
     to_sib(1, blk_r, LO)
     to_sib(2, blk_l, HI)
     for h in HALVES:
         to_sib(3, head, h)
     cs_r[...] = both(1, blk_r, LO)
     cs_l[...] = both(2, blk_l, HI)
-    links.arrive(k_or, r_opp.at[LO], left)
-    s_right[LO] = (cs_r[...] + r_opp[LO].astype(F32)).astype(BF16)
-    links.send(k_er + LO, s_right.at[LO], r_left.at[LO], right)
-    links.arrive(k_ol, r_opp.at[HI], right)
-    s_left[HI] = (cs_l[...] + r_opp[HI].astype(F32)).astype(BF16)
-    links.send(k_el + HI, s_left.at[HI], r_right.at[HI], left)
+    for i, rows in enumerate(parts):
+        links.arrive(k_or + i, r_opp.at[LO, rows], left)
+        s_right[LO, rows] = (cs_r[rows, :] + r_opp[LO, rows].astype(F32)).astype(BF16)
+        links.send(k_er + i, s_right.at[LO, rows], r_left.at[LO, rows], right)
+        links.arrive(k_ol + i, r_opp.at[HI, rows], right)
+        s_left[HI, rows] = (cs_l[rows, :] + r_opp[HI, rows].astype(F32)).astype(BF16)
+        links.send(k_el + i, s_left.at[HI, rows], r_right.at[HI, rows], left)
     for h in HALVES:
         outv[h] = both(3, head, h)
-    links.arrive(k_el + LO, r_right.at[LO], right)
+    links.arrive(k_el + 2, r_right.at[LO], right)
     outv[LO] = outv[LO] + r_right[LO].astype(F32)
-    links.arrive(k_er + HI, r_left.at[HI], left)
+    links.arrive(k_er + 2, r_left.at[HI], left)
     outv[HI] = outv[HI] + r_left[HI].astype(F32)
-    links.arrive(k_er + LO, r_left.at[LO], left)
-    out[:, :half] = outv[LO] + r_left[LO].astype(F32)
-    links.arrive(k_el + HI, r_right.at[HI], right)
-    out[:, half:] = outv[HI] + r_right[HI].astype(F32)
+    for i, rows in enumerate(parts):
+        links.arrive(k_er + i, r_left.at[LO, rows], left)
+        out[rows, :half] = outv[LO, rows] + r_left[LO, rows].astype(F32)
+        links.arrive(k_el + i, r_right.at[HI, rows], right)
+        out[rows, half:] = outv[HI, rows] + r_right[HI, rows].astype(F32)
 
     def sent_f(d, carry):
         links.make(k_g + d, f_tot, f_tot, dev_g(1)).wait_send()

time: 51 us -> 51 us (level)
  no operation moved by 1% of the time
where the time goes in v5:
time: 51 us; the launch traced here: 50.9 us
  Pallas kernels  50.1 us (98%)
  local copies, waits for them, and re-layouts  0.8 us (2%)
    pallas_call x1, Pallas kernels, local(): pl.pallas_call(functools.partial(kernel, nz, ny), out_shape=pltpu.VMEM((t...  50.1 us

profile of v5, /device:TPU:1, one launch (start us, length us, event | category | flops | bytes accessed | tf_op | source)
XLA Modules:
  0.0 50.9 jit_solution(10159625573604047193)
XLA Ops:
  0.0 50.1 %shard_map.100 = f32[256,512]{1,0:T(8,128)S(1)} custom-call(bf16[256,512]{1,0:T(8,128)(2,1)} %emb_h.1, bf16[256,512]{1,0:T(8,128)(2,1)} %noise_h.1, bf16[8,512,512]{2,1,0:T(8,128)(2,1)} %bitcast.5, bf16[8,512,512]{2,1,0:T(8,128)(2,1)} %bitcast.6, f32[256,128]{1,0:T(8,128)} %b_h.1, f32[256,128]{1,0:T(8,128)} %c_h.1, f32[8,256]{1,0:T(8,128)} %ld_h.1, ...), custom_call_target="tpu_custom_call" | custom-call | flops 4294967296 | bytes 10485760 | tf_op jit(solution)/shard_map/pallas_call | solution.py:614
  50.1 0.8 %copy.12 = f32[256,512]{1,0:T(8,128)} copy(f32[256,512]{1,0:T(8,128)S(1)} %shard_map.100) | data formatting | bytes 1048576

commit v6 on v4

--- a/solution.py
+++ b/solution.py
@@ -452,18 +452,16 @@
     b_all, c_all = bv[...].astype(BF16), cv[...].astype(BF16)
     for d in range(1, NG):
         links.arrive(k_bf + d, f_in.at[at_m(NG - d)], dev_m(d))
-    for q in range(NX):
-        span = quarter(q)
-        out_y = y_loc[:, span] + dec_in[:, span] * dot(c_all, whole(f_in, q))
-        gz[:, span] = (fz[:, span] * out_y).astype(BF16)
+    entered = jnp.concatenate([whole(f_in, q) for q in range(NX)], axis=1)
+    out_y = y_loc[...] + dec_in[...] * dot(c_all, entered)
+    gz[...] = (fz[...] * out_y).astype(BF16)
     for i, blk in enumerate((blk_o + other, blk_o)):
         for h in HALVES:
             early[2 * i + h] = dot_t(gz[...], wz[blk, h * half : (h + 1) * half, :])
     for d in range(1, NG):
         links.arrive(k_bb + d, b_in.at[at_m(NG - d)], dev_m(d))
-    for q in range(NX):
-        span = quarter(q)
-        gx[:, span] = (gx_loc[:, span] + dec_out[:, span] * dot(b_all, whole(b_in, q))).astype(BF16)
+    entered = jnp.concatenate([whole(b_in, q) for q in range(NX)], axis=1)
+    gx[...] = (gx_loc[...] + dec_out[...] * dot(b_all, entered)).astype(BF16)
 
     def share(blk, h, done):
         span = slice(h * half, (h + 1) * half)

time: 51 us -> 51 us (level)
  no operation moved by 1% of the time
where the time goes in v6:
time: 51 us; the launch traced here: 50.9 us
  Pallas kernels  50.1 us (98%)
  local copies, waits for them, and re-layouts  0.8 us (2%)
    pallas_call x1, Pallas kernels, local(): pl.pallas_call(functools.partial(kernel, nz, ny), out_shape=pltpu.VMEM((t...  50.1 us

profile of v6, /device:TPU:1, one launch (start us, length us, event | category | flops | bytes accessed | tf_op | source)
XLA Modules:
  0.0 50.9 jit_solution(4048225037887688798)
XLA Ops:
  0.0 50.1 %shard_map.100 = f32[256,512]{1,0:T(8,128)S(1)} custom-call(bf16[256,512]{1,0:T(8,128)(2,1)} %emb_h.1, bf16[256,512]{1,0:T(8,128)(2,1)} %noise_h.1, bf16[8,512,512]{2,1,0:T(8,128)(2,1)} %bitcast.5, bf16[8,512,512]{2,1,0:T(8,128)(2,1)} %bitcast.6, f32[256,128]{1,0:T(8,128)} %b_h.1, f32[256,128]{1,0:T(8,128)} %c_h.1, f32[8,256]{1,0:T(8,128)} %ld_h.1, ...), custom_call_target="tpu_custom_call" | custom-call | flops 4294967296 | bytes 10485760 | tf_op jit(solution)/shard_map/pallas_call | solution.py:609
  50.1 0.8 %copy.12 = f32[256,512]{1,0:T(8,128)} copy(f32[256,512]{1,0:T(8,128)S(1)} %shard_map.100) | data formatting | bytes 1048576
